TPU v7x, 256 devices: a whole 4x4x8 slice. The times are simulated.
256 devices in a mesh: gx: 16 (over x, z_hi), gy: 4 (over y), gz: 4 (over z_lo, core).
Axes of the slice: x: 4, y: 4, z: 8 (z_hi: 4, z_lo: 2; z = z_hi * 2 + z_lo), core: 2. Of those that a mesh axis runs over, the one named last changes fastest.
Arguments:
- solid_state: float32 [9, 32, 128, 512], P(None, 'gz', 'gx', 'gy'), may hold values from -6 to 6
- material: float32 [4, 32, 128, 512], P(None, 'gz', 'gx', 'gy'), may hold values from 0.5 to 2
- ocean_state: float32 [4, 16, 256, 1024], P(None, None, 'gx', ('gy', 'gz')), may hold values from -6 to 6
- ocean_medium: float32 [2, 16], replicated, may hold values from 0.5 to 2
- offset_x: int32 [256], P('gx'), may hold values from -1 to 1
- offset_y: int32 [1024], P(('gy', 'gz')), may hold values from -1 to 1
Outputs:
- solid_next: float32 [9, 32, 128, 512], P(None, 'gz', 'gx', 'gy')
- solid_rate: float32 [9, 32, 128, 512], P(None, 'gz', 'gx', 'gy')
- ocean_next: float32 [4, 16, 256, 1024], P(None, None, 'gx', ('gy', 'gz'))
- ocean_rate: float32 [4, 16, 256, 1024], P(None, None, 'gx', ('gy', 'gz'))
All inputs are finite; a program needn't handle non-finite values.
Results may differ from a plain program's by a relative error of at most 0.000059.
Values sent between devices are 32-bit elements; how exact they have to be, the bound alone decides.
A program may use at most 64 MiB of HBM per device.

v0:
```python
import jax
import jax.numpy as jnp
from jax import lax
from jax.sharding import PartitionSpec as P

closure_rows = (
    (-24.0 / 17.0, 59.0 / 34.0, -4.0 / 17.0, -3.0 / 34.0, 0.0, 0.0),
    (-0.5, 0.0, 0.5, 0.0, 0.0, 0.0),
    (4.0 / 43.0, -59.0 / 86.0, 0.0, 59.0 / 86.0, -4.0 / 43.0, 0.0),
    (3.0 / 98.0, 0.0, -59.0 / 98.0, 0.0, 32.0 / 49.0, -4.0 / 49.0),
)
inv_norm = 48.0 / 17.0
step_size = 0.25
section_weight = 0.1496590219993
gravity = 0.4


def with_halo(x, sides, width):
    for axis, dim in sides:
        size, length = (lax.axis_size(axis), x.shape[dim])
        up = [(i, (i + 1) % size) for i in range(size - 1)]
        down = [(j, i) for i, j in up]
        last = lax.slice_in_dim(x, length - width, length, axis=dim)
        leading = lax.slice_in_dim(x, 0, width, axis=dim)
        before = lax.ppermute(last, axis, up)
        after = lax.ppermute(leading, axis, down)
        x = jnp.concatenate([before, x, after], axis=dim)
    return x


def broadcast(block, axis, owner):
    block = jnp.where(lax.axis_index(axis) == owner, block, jnp.zeros_like(block))
    return lax.psum(block, axis)


def take_slab(field, first_index, length, dimension):
    return lax.slice_in_dim(field, first_index, first_index + length, axis=dimension)


def closure(field, dimension, at_end):
    extent = field.shape[dimension]
    pieces = []
    for row_index in range(4):
        running = jnp.zeros_like(take_slab(field, 0, 1, dimension))
        for col_index in range(6):
            weight = closure_rows[row_index][col_index]
            if weight != 0.0:
                if at_end:
                    running = running - weight * take_slab(
                        field, extent - 1 - col_index, 1, dimension
                    )
                else:
                    running = running + weight * take_slab(field, col_index, 1, dimension)
        pieces.append(running)
    if at_end:
        pieces = pieces[::-1]
    return jnp.concatenate(pieces, axis=dimension)


def interior(padded, dimension, extent):
    return (
        take_slab(padded, 0, extent, dimension)
        - 8.0 * take_slab(padded, 1, extent, dimension)
        + 8.0 * take_slab(padded, 3, extent, dimension)
        - take_slab(padded, 4, extent, dimension)
    ) / 12.0


def derivative(field, dimension):
    extent = field.shape[dimension]
    widths = [(0, 0)] * field.ndim
    widths[dimension] = (2, 2)
    middle = interior(jnp.pad(field, widths), dimension, extent)
    return jnp.concatenate(
        [
            closure(field, dimension, False),
            take_slab(middle, 4, extent - 8, dimension),
            closure(field, dimension, True),
        ],
        axis=dimension,
    )


def local_derivative(padded, field, dimension, is_first, is_last):
    extent = field.shape[dimension]
    middle = interior(padded, dimension, extent)
    head = jnp.where(is_first, closure(field, dimension, False), take_slab(middle, 0, 4, dimension))
    tail = jnp.where(
        is_last, closure(field, dimension, True), take_slab(middle, extent - 4, 4, dimension)
    )
    return jnp.concatenate(
        [head, take_slab(middle, 4, extent - 8, dimension), tail], axis=dimension
    )


def blend_matrix(offsets, fine_first, coarse_first, columns, coarse_total):
    fine_index = fine_first + jnp.arange(offsets.shape[0], dtype=jnp.int32)
    coarse = fine_index // 2
    target = jnp.clip(coarse + offsets, 0, coarse_total - 1)
    column = jnp.arange(columns, dtype=jnp.int32)[None, :]
    nearest = (column == (coarse - coarse_first)[:, None]).astype(jnp.float32)
    farther = (column == (target - coarse_first)[:, None]).astype(jnp.float32)
    return 0.75 * nearest + 0.25 * farther


def restrict(bottom):
    fine_rows, fine_cols = bottom.shape
    return bottom.reshape(fine_rows // 2, 2, fine_cols // 2, 2).mean(axis=(1, 3))


def solid_rates(material, diff_x, diff_y, diff_z):
    buoyancy = material[0]
    lame_one = material[1]
    lame_two = material[2]
    metric = material[3]

    def vertical(member):
        return metric * diff_z(member)

    strain_xx = diff_x(0)
    strain_yy = diff_y(1)
    strain_zz = vertical(2)
    dilation = strain_xx + strain_yy + strain_zz
    return [
        buoyancy * (diff_x(3) + diff_y(8) + vertical(7)),
        buoyancy * (diff_x(8) + diff_y(4) + vertical(6)),
        buoyancy * (diff_x(7) + diff_y(6) + vertical(5)),
        lame_one * dilation + 2.0 * lame_two * strain_xx,
        lame_one * dilation + 2.0 * lame_two * strain_yy,
        lame_one * dilation + 2.0 * lame_two * strain_zz,
        lame_two * (vertical(1) + diff_y(2)),
        lame_two * (vertical(0) + diff_x(2)),
        lame_two * (diff_y(0) + diff_x(1)),
    ]


def seafloor_terms(state, material, bed_pressure):
    factor = inv_norm * material[0, 0] * material[3, 0]
    return (factor * state[7, 0], factor * state[6, 0], factor * (state[5, 0] + bed_pressure))


def ocean_rates(state, medium, diff_x, diff_y, bed_speed):
    bulk = medium[0][:, None, None]
    light = medium[1][:, None, None]
    pressure = state[0]
    flow_z = state[3]
    rate_p = (
        -bulk * (2.0 * diff_x(1) + 2.0 * diff_y(2) + derivative(flow_z, 0))
        + gravity * flow_z / light
    )
    rate_p = rate_p.at[-1].add(inv_norm * bulk[-1] * (flow_z[-1] - bed_speed))
    rate_u = -2.0 * light * diff_x(0)
    rate_v = -2.0 * light * diff_y(0)
    rate_w = -light * derivative(pressure, 0)
    rate_w = rate_w.at[0].add(-inv_norm * light[0] * pressure[0])
    return jnp.stack([rate_p, rate_u, rate_v, rate_w])


def body(solid_state, material, ocean_state, ocean_medium, offset_x, offset_y):
    highest = lax.Precision.HIGHEST
    span_x = lax.axis_size("gx")
    span_y = lax.axis_size("gy")
    span_z = lax.axis_size("gz")
    index_x = lax.axis_index("gx")
    index_y = lax.axis_index("gy")
    index_z = lax.axis_index("gz")
    cells_x = solid_state.shape[2]
    cells_y = solid_state.shape[3]
    column_width = ocean_state.shape[3]
    x_first = index_x == 0
    x_last = index_x == span_x - 1
    y_first = index_y == 0
    y_last = index_y == span_y - 1
    z_first = index_z == 0
    z_last = index_z == span_z - 1
    joint_first = jnp.logical_and(y_first, z_first)
    joint_last = jnp.logical_and(y_last, z_last)
    plane = solid_state[2, 0]
    rimmed = with_halo(plane, (("gx", 0), ("gy", 1)), 1)
    shared = broadcast(rimmed, "gz", 0)
    bottom_part = restrict(ocean_state[0, -1])
    bed_pressure = lax.all_gather(bottom_part, "gz", axis=1, tiled=True)
    ocean_rim = with_halo(ocean_state[0:3], (("gx", 2), (("gy", "gz"), 3)), 2)
    padded = with_halo(solid_state, (("gx", 2), ("gy", 3), ("gz", 1)), 2)

    def padded_x(member):
        return padded[member, 2:-2, :, 2:-2]

    def padded_y(member):
        return padded[member, 2:-2, 2:-2, :]

    def padded_z(member):
        return padded[member, :, 2:-2, 2:-2]

    rates = solid_rates(
        material,
        lambda member: local_derivative(padded_x(member), solid_state[member], 1, x_first, x_last),
        lambda member: local_derivative(padded_y(member), solid_state[member], 2, y_first, y_last),
        lambda member: local_derivative(padded_z(member), solid_state[member], 0, z_first, z_last),
    )
    term_x, term_y, term_z = seafloor_terms(solid_state, material, bed_pressure)
    rates[0] = rates[0].at[0].add(jnp.where(z_first, term_x, 0.0))
    rates[1] = rates[1].at[0].add(jnp.where(z_first, term_y, 0.0))
    rates[2] = rates[2].at[0].add(jnp.where(z_first, term_z, 0.0))
    solid_rate = step_size * jnp.stack(rates)
    solid_next = solid_state + section_weight * solid_rate
    blend_x = blend_matrix(
        offset_x, index_x * 2 * cells_x, index_x * cells_x - 1, cells_x + 2, cells_x * span_x
    )
    blend_y = blend_matrix(
        offset_y,
        index_y * 2 * cells_y + index_z * column_width,
        index_y * cells_y - 1,
        cells_y + 2,
        cells_y * span_y,
    )
    bed_speed = jnp.dot(jnp.dot(blend_x, shared, precision=highest), blend_y.T, precision=highest)
    ocean_rate = step_size * ocean_rates(
        ocean_state,
        ocean_medium,
        lambda member: local_derivative(
            ocean_rim[member, :, :, 2:-2], ocean_state[member], 1, x_first, x_last
        ),
        lambda member: local_derivative(
            ocean_rim[member, :, 2:-2, :], ocean_state[member], 2, joint_first, joint_last
        ),
        bed_speed,
    )
    ocean_next = ocean_state + section_weight * ocean_rate
    return (solid_next, solid_rate, ocean_next, ocean_rate)


def solution(mesh):
    in_specs = (
        P(None, "gz", "gx", "gy"),
        P(None, "gz", "gx", "gy"),
        P(None, None, "gx", ("gy", "gz")),
        P(),
        P("gx"),
        P(("gy", "gz")),
    )
    out_specs = (
        P(None, "gz", "gx", "gy"),
        P(None, "gz", "gx", "gy"),
        P(None, None, "gx", ("gy", "gz")),
        P(None, None, "gx", ("gy", "gz")),
    )
    return jax.shard_map(body, mesh=mesh, in_specs=in_specs, out_specs=out_specs, check_vma=False)
```

profile of v0, /device:TPU:15, one launch (start us, length us, event | category | flops | bytes accessed | tf_op | source)
XLA Modules:
  0.0 215.0 jit_solution(1895889747051909236)
XLA Ops:
  0.6 1.7 fusion.202
  2.3 4.9 %collective-permute-start.6 = (f32[3,16,2,64]{3,2,1,0:T(2,128)}, f32[3,16,2,64]{3,2,1,0:T(2,128)S(1)}, u32[]{:S(2)}, u32[]{:S(2)}) collective-permute-start(f32[3,16,2,64]{3,2,1,0:T(2,128)} %get-tuple-element.132), channel_id=1, source_target_pairs={{0,16},{16,32},{32,48},{48,64},{64,80},{80,96},{96,112},{112,128},... | collective-permute-start | bytes 73736 | tf_op jit(solution)/shard_map/ppermute | solution.py:25
  7.2 5.2 %collective-permute-start.7 = (f32[3,16,2,64]{3,2,1,0:T(2,128)}, f32[3,16,2,64]{3,2,1,0:T(2,128)S(1)}, u32[]{:S(2)}, u32[]{:S(2)}) collective-permute-start(f32[3,16,2,64]{3,2,1,0:T(2,128)} %get-tuple-element.133), channel_id=1, source_target_pairs={{16,0},{32,16},{48,32},{64,48},{80,64},{96,80},{112,96},{128,112},... | collective-permute-start | bytes 73736 | tf_op jit(solution)/shard_map/ppermute | solution.py:26
  12.4 1.3 slice_bitcast_fusion.34
  13.8 2.8 %collective-permute-start.10 = (f32[1,128]{1,0:T(1,128)}, f32[1,128]{1,0:T(1,128)}, u32[]{:S(2)}, u32[]{:S(2)}) collective-permute-start(f32[1,128]{1,0:T(1,128)} %get-tuple-element.140), channel_id=1, source_target_pairs={{0,16},{16,32},{32,48},{48,64},{64,80},{80,96},{96,112},{112,128},... | collective-permute-start | bytes 1544 | tf_op jit(solution)/shard_map/ppermute | solution.py:25
  16.6 5.5 %collective-permute-start.11 = (f32[1,128]{1,0:T(1,128)}, f32[1,128]{1,0:T(1,128)}, u32[]{:S(2)}, u32[]{:S(2)}) collective-permute-start(f32[1,128]{1,0:T(1,128)} %get-tuple-element.141), channel_id=1, source_target_pairs={{16,0},{32,16},{48,32},{64,48},{80,64},{96,80},{112,96},{128,112},... | collective-permute-start | bytes 1544 | tf_op jit(solution)/shard_map/ppermute | solution.py:26
  22.1 1.8 fusion.203
  23.8 1.9 collective-permute-start
  26.8 1.5 slice_multiply_fusion.35
  55.7 1.1 copy.1215
  56.8 1.1 copy.1217
  57.8 1.1 copy.1219
  58.9 1.1 copy.1226
  60.0 1.1 copy.1227
  61.0 1.1 copy.1229
  63.9 1.1 copy.1222
  78.8 1.3 slice.2867
  80.1 1.2 slice.2868
  84.2 6.8 %all-gather = f32[4,32,8]{1,2,0:T(8,128)S(1)} all-gather(f32[1,32,8]{1,2,0:T(8,128)S(1)} %multiply_bitcast_fusion), channel_id=1, replica_groups=mesh['gx'=16,'gy'=4,'gz'=4] {'gz'}, dimensions={0}, use_global_device_ids=true | all-gather | bytes 5120 | tf_op jit(solution)/shard_map/all_gather | solution.py:182
  99.9 1.3 clamp_subtract_fusion
  101.9 1.3 add_add_fusion.6
  107.3 6.4 %collective-permute-start.1 = (f32[9,8,2,128]{3,2,1,0:T(2,128)}, f32[9,8,2,128]{3,2,1,0:T(2,128)S(1)}, u32[]{:S(2)}, u32[]{:S(2)}) collective-permute-start(f32[9,8,2,128]{3,2,1,0:T(2,128)} %get-tuple-element.204), channel_id=1, source_target_pairs={{16,0},{32,16},{48,32},{64,48},{80,64},{96,80},{112,96},{128,112},... | collective-permute-start | bytes 221192 | tf_op jit(solution)/shard_map/ppermute | solution.py:26
  114.4 3.2 %collective-permute-start.12 = (f32[10,1]{1,0:T(8,128)S(1)}, f32[10,1]{1,0:T(8,128)S(1)}, u32[]{:S(2)}, u32[]{:S(2)}) collective-permute-start(f32[10,1]{1,0:T(8,128)S(1)} %get-tuple-element.484), channel_id=1, source_target_pairs={{0,4},{4,8},{8,12},{1,5},{5,9},{9,13},{2,6},{6,10},{10,14},{3,7},{... | collective-permute-start | bytes 128 | tf_op jit(solution)/shard_map/ppermute | solution.py:25
  117.6 1.2 collective-permute-done.12
  118.8 1.9 collective-permute-start.13
  120.7 2.5 %collective-permute-done.13 = f32[10,1]{1,0:T(8,128)S(1)} collective-permute-done((f32[10,1]{1,0:T(8,128)S(1)}, f32[10,1]{1,0:T(8,128)S(1)}, u32[]{:S(2)}, u32[]{:S(2)}) %collective-permute-start.13) | collective-permute-done | bytes 72 | tf_op jit(solution)/shard_map/ppermute | solution.py:26
  123.9 11.3 %psum.7 = f32[10,130]{1,0:T(8,128)S(1)} all-reduce(f32[10,130]{1,0:T(8,128)S(1)} %maximum_select_fusion.3), channel_id=1, replica_groups=mesh['gx'=16,'gy'=4,'gz'=4] {'gz'}, use_global_device_ids=true, to_apply=%region_1.2 | all-reduce | flops 1300 | bytes 10400 | tf_op jit(solution)/shard_map/psum | solution.py:33
  137.6 4.2 %collective-permute-start.8 = (f32[3,16,20,2]{2,1,3,0:T(8,128)}, f32[3,16,20,2]{2,1,3,0:T(8,128)S(1)}, u32[]{:S(2)}, u32[]{:S(2)}) collective-permute-start(f32[3,16,20,2]{2,1,3,0:T(8,128)} %copy.1199), channel_id=1, source_target_pairs={{0,1},{1,2},{2,3},{3,4},{4,5},{5,6},{6,7},{7,8},{8,9},{9,10},{10,1... | collective-permute-start | bytes 23048 | tf_op jit(solution)/shard_map/ppermute | solution.py:25
  142.3 2.1 collective-permute-start.9
  145.7 2.0 collective-permute-done.9
  149.7 1.5 slice_multiply_fusion.23
  153.0 2.1 fusion.4
  156.0 1.7 copy.1288
  157.6 1.7 copy.1283
  159.3 1.7 copy.1284
  160.9 1.7 copy.1286
  162.6 1.7 copy.1291
  164.2 1.7 copy.1292
  165.9 1.7 copy.1294
  167.6 1.7 copy.1296
  169.2 1.7 copy.1299
  170.9 1.7 copy.1300
  172.6 1.7 copy.1303
  185.5 3.2 %collective-permute-start.2 = (f32[9,8,12,2]{2,1,3,0:T(8,128)S(1)}, f32[9,8,12,2]{2,1,3,0:T(8,128)S(1)}, u32[]{:S(2)}, u32[]{:S(2)}) collective-permute-start(f32[9,8,12,2]{2,1,3,0:T(8,128)S(1)} %copy.917), channel_id=1, source_target_pairs={{0,4},{4,8},{8,12},{1,5},{5,9},{9,13},{2,6},{6,10},{10,14},{3,7},{... | collective-permute-start | bytes 20744 | tf_op jit(solution)/shard_map/ppermute | solution.py:25
  189.6 2.1 collective-permute-start.3
  196.5 3.7 %collective-permute-start.4 = (f32[9,2,12,132]{3,2,1,0:T(8,128)S(1)}, f32[9,2,12,132]{3,2,1,0:T(8,128)S(1)}, u32[]{:S(2)}, u32[]{:S(2)}) collective-permute-start(f32[9,2,12,132]{3,2,1,0:T(8,128)S(1)} %get-tuple-element.112), channel_id=1, source_target_pairs={{0,1},{1,2},{2,3},{4,5},{5,6},{6,7},{8,9},{9,10},{10,11},{12,13},{... | collective-permute-start | bytes 342152 | tf_op jit(solution)/shard_map/ppermute | solution.py:25
  200.1 2.1 collective-permute-start.5
  205.9 2.2 %collective-permute-done.5 = f32[9,2,12,132]{3,2,1,0:T(8,128)S(1)} collective-permute-done((f32[9,2,12,132]{3,2,1,0:T(8,128)S(1)}, f32[9,2,12,132]{3,2,1,0:T(8,128)S(1)}, u32[]{:S(2)}, u32[]{:S(2)}) %collective-permute-start.5) | collective-permute-done | bytes 114080 | tf_op jit(solution)/shard_map/ppermute | solution.py:26
  (731 shorter events, 93.9 us)
Async XLA Ops:
  2.3 133.6 %collective-permute-start.6 = (f32[3,16,2,64]{3,2,1,0:T(2,128)}, f32[3,16,2,64]{3,2,1,0:T(2,128)S(1)}, u32[]{:S(2)}, u32[]{:S(2)}) collective-permute-start(f32[3,16,2,64]{3,2,1,0:T(2,128)} %get-tuple-element.132), channel_id=1, source_target_pairs={{0,16},{16,32},{32,48},{48,64},{64,80},{80,96},{96,112},{112,128},... | collective-permute-start | bytes 73736 | tf_op jit(solution)/shard_map/ppermute | solution.py:25
  7.2 128.7 %collective-permute-start.7 = (f32[3,16,2,64]{3,2,1,0:T(2,128)}, f32[3,16,2,64]{3,2,1,0:T(2,128)S(1)}, u32[]{:S(2)}, u32[]{:S(2)}) collective-permute-start(f32[3,16,2,64]{3,2,1,0:T(2,128)} %get-tuple-element.133), channel_id=1, source_target_pairs={{16,0},{32,16},{48,32},{64,48},{80,64},{96,80},{112,96},{128,112},... | collective-permute-start | bytes 73736 | tf_op jit(solution)/shard_map/ppermute | solution.py:26
  13.8 93.5 %collective-permute-start.10 = (f32[1,128]{1,0:T(1,128)}, f32[1,128]{1,0:T(1,128)}, u32[]{:S(2)}, u32[]{:S(2)}) collective-permute-start(f32[1,128]{1,0:T(1,128)} %get-tuple-element.140), channel_id=1, source_target_pairs={{0,16},{16,32},{32,48},{48,64},{64,80},{80,96},{96,112},{112,128},... | collective-permute-start | bytes 1544 | tf_op jit(solution)/shard_map/ppermute | solution.py:25
  16.6 97.1 %collective-permute-start.11 = (f32[1,128]{1,0:T(1,128)}, f32[1,128]{1,0:T(1,128)}, u32[]{:S(2)}, u32[]{:S(2)}) collective-permute-start(f32[1,128]{1,0:T(1,128)} %get-tuple-element.141), channel_id=1, source_target_pairs={{16,0},{32,16},{48,32},{64,48},{80,64},{96,80},{112,96},{128,112},... | collective-permute-start | bytes 1544 | tf_op jit(solution)/shard_map/ppermute | solution.py:26
  23.8 160.8 %collective-permute-start = (f32[9,8,2,128]{3,2,1,0:T(2,128)}, f32[9,8,2,128]{3,2,1,0:T(2,128)S(1)}, u32[]{:S(2)}, u32[]{:S(2)}) collective-permute-start(f32[9,8,2,128]{3,2,1,0:T(2,128)} %get-tuple-element.203), channel_id=1, source_target_pairs={{0,16},{16,32},{32,48},{48,64},{64,80},{80,96},{96,112},{112,128},... | collective-permute-start | bytes 221192 | tf_op jit(solution)/shard_map/ppermute | solution.py:25
  72.5 21.7 %copy-start.55 = (f32[8,8,1]{2,1,0:T(8,128)S(1)}, f32[8,8,1]{2,1,0:T(8,128)}, u32[]{:S(2)}) copy-start(f32[8,8,1]{2,1,0:T(8,128)} %get-tuple-element.402) | copy-start | bytes 772
  74.3 23.7 %copy-start.47 = (f32[8,8,1]{2,1,0:T(8,128)S(1)}, f32[8,8,1]{2,1,0:T(8,128)}, u32[]{:S(2)}) copy-start(f32[8,8,1]{2,1,0:T(8,128)} %get-tuple-element.412) | copy-start | bytes 772
  74.3 23.7 %copy-start.48 = (f32[8,8,1]{2,1,0:T(8,128)S(1)}, f32[8,8,1]{2,1,0:T(8,128)}, u32[]{:S(2)}) copy-start(f32[8,8,1]{2,1,0:T(8,128)} %get-tuple-element.415) | copy-start | bytes 772
  75.0 23.7 %copy-start.117 = (f32[8,1,128]{2,1,0:T(1,128)S(1)}, f32[8,1,128]{2,1,0:T(1,128)}, u32[]{:S(2)}) copy-start(f32[8,1,128]{2,1,0:T(1,128)} %get-tuple-element.390) | copy-start | bytes 12292
  75.0 23.7 %copy-start.156 = (f32[8,1,128]{2,1,0:T(1,128)S(1)}, f32[8,1,128]{2,1,0:T(1,128)}, u32[]{:S(2)}) copy-start(f32[8,1,128]{2,1,0:T(1,128)} %get-tuple-element.394) | copy-start | bytes 12292
  75.0 26.2 %copy-start.62 = (f32[8,8,1]{2,1,0:T(8,128)S(1)}, f32[8,8,1]{2,1,0:T(8,128)}, u32[]{:S(2)}) copy-start(f32[8,8,1]{2,1,0:T(8,128)} %get-tuple-element.400) | copy-start | bytes 772
  75.0 26.2 %copy-start.63 = (f32[8,8,1]{2,1,0:T(8,128)S(1)}, f32[8,8,1]{2,1,0:T(8,128)}, u32[]{:S(2)}) copy-start(f32[8,8,1]{2,1,0:T(8,128)} %get-tuple-element.401) | copy-start | bytes 772
  75.0 26.2 %copy-start.64 = (f32[8,8,1]{2,1,0:T(8,128)S(1)}, f32[8,8,1]{2,1,0:T(8,128)}, u32[]{:S(2)}) copy-start(f32[8,8,1]{2,1,0:T(8,128)} %get-tuple-element.403) | copy-start | bytes 772
  75.6 26.2 %copy-start.118 = (f32[8,1,128]{2,1,0:T(1,128)S(1)}, f32[8,1,128]{2,1,0:T(1,128)}, u32[]{:S(2)}) copy-start(f32[8,1,128]{2,1,0:T(1,128)} %get-tuple-element.365) | copy-start | bytes 12292
  75.6 27.5 %copy-start.154 = (f32[8,1,128]{2,1,0:T(1,128)S(1)}, f32[8,1,128]{2,1,0:T(1,128)}, u32[]{:S(2)}) copy-start(f32[8,1,128]{2,1,0:T(1,128)} %get-tuple-element.332) | copy-start | bytes 12292
  75.6 27.5 %copy-start.155 = (f32[8,1,128]{2,1,0:T(1,128)S(1)}, f32[8,1,128]{2,1,0:T(1,128)}, u32[]{:S(2)}) copy-start(f32[8,1,128]{2,1,0:T(1,128)} %get-tuple-element.391) | copy-start | bytes 12292
  75.6 27.5 %copy-start.185 = (f32[8,1,128]{2,1,0:T(1,128)S(1)}, f32[8,1,128]{2,1,0:T(1,128)}, u32[]{:S(2)}) copy-start(f32[8,1,128]{2,1,0:T(1,128)} %get-tuple-element.334) | copy-start | bytes 12292
  75.6 27.5 %copy-start.186 = (f32[8,1,128]{2,1,0:T(1,128)S(1)}, f32[8,1,128]{2,1,0:T(1,128)}, u32[]{:S(2)}) copy-start(f32[8,1,128]{2,1,0:T(1,128)} %get-tuple-element.393) | copy-start | bytes 12292
  76.3 27.5 %copy-start.200 = (f32[8,1,128]{2,1,0:T(1,128)S(1)}, f32[8,1,128]{2,1,0:T(1,128)}, u32[]{:S(2)}) copy-start(f32[8,1,128]{2,1,0:T(1,128)} %get-tuple-element.354) | copy-start | bytes 12292
  76.3 27.5 %copy-start.201 = (f32[8,1,128]{2,1,0:T(1,128)S(1)}, f32[8,1,128]{2,1,0:T(1,128)}, u32[]{:S(2)}) copy-start(f32[8,1,128]{2,1,0:T(1,128)} %get-tuple-element.355) | copy-start | bytes 12292
  76.3 27.5 %copy-start.202 = (f32[8,1,128]{2,1,0:T(1,128)S(1)}, f32[8,1,128]{2,1,0:T(1,128)}, u32[]{:S(2)}) copy-start(f32[8,1,128]{2,1,0:T(1,128)} %get-tuple-element.358) | copy-start | bytes 12292
  76.3 27.5 %copy-start.203 = (f32[8,1,128]{2,1,0:T(1,128)S(1)}, f32[8,1,128]{2,1,0:T(1,128)}, u32[]{:S(2)}) copy-start(f32[8,1,128]{2,1,0:T(1,128)} %get-tuple-element.359) | copy-start | bytes 12292
  76.3 27.5 %copy-start.204 = (f32[8,1,128]{2,1,0:T(1,128)S(1)}, f32[8,1,128]{2,1,0:T(1,128)}, u32[]{:S(2)}) copy-start(f32[8,1,128]{2,1,0:T(1,128)} %get-tuple-element.361) | copy-start | bytes 12292
  77.5 26.9 %copy-start.17 = (f32[8,8,1]{2,1,0:T(8,128)S(1)}, f32[8,8,1]{2,1,0:T(8,128)}, u32[]{:S(2)}) copy-start(f32[8,8,1]{2,1,0:T(8,128)} %get-tuple-element.371) | copy-start | bytes 772
  77.5 26.9 %copy-start.18 = (f32[8,8,1]{2,1,0:T(8,128)S(1)}, f32[8,8,1]{2,1,0:T(8,128)}, u32[]{:S(2)}) copy-start(f32[8,8,1]{2,1,0:T(8,128)} %get-tuple-element.373) | copy-start | bytes 772
  77.5 26.9 %copy-start.19 = (f32[8,8,1]{2,1,0:T(8,128)S(1)}, f32[8,8,1]{2,1,0:T(8,128)}, u32[]{:S(2)}) copy-start(f32[8,8,1]{2,1,0:T(8,128)} %get-tuple-element.374) | copy-start | bytes 772
  77.5 26.9 %copy-start.20 = (f32[8,8,1]{2,1,0:T(8,128)S(1)}, f32[8,8,1]{2,1,0:T(8,128)}, u32[]{:S(2)}) copy-start(f32[8,8,1]{2,1,0:T(8,128)} %get-tuple-element.375) | copy-start | bytes 772
  77.5 27.0 %copy-start.21 = (f32[8,8,1]{2,1,0:T(8,128)S(1)}, f32[8,8,1]{2,1,0:T(8,128)}, u32[]{:S(2)}) copy-start(f32[8,8,1]{2,1,0:T(8,128)} %get-tuple-element.376) | copy-start | bytes 772
  77.5 27.0 %copy-start.22 = (f32[8,8,1]{2,1,0:T(8,128)S(1)}, f32[8,8,1]{2,1,0:T(8,128)}, u32[]{:S(2)}) copy-start(f32[8,8,1]{2,1,0:T(8,128)} %get-tuple-element.377) | copy-start | bytes 772
  77.5 27.0 %copy-start.23 = (f32[8,8,1]{2,1,0:T(8,128)S(1)}, f32[8,8,1]{2,1,0:T(8,128)}, u32[]{:S(2)}) copy-start(f32[8,8,1]{2,1,0:T(8,128)} %get-tuple-element.378) | copy-start | bytes 772
  77.5 27.0 %copy-start.24 = (f32[8,8,1]{2,1,0:T(8,128)S(1)}, f32[8,8,1]{2,1,0:T(8,128)}, u32[]{:S(2)}) copy-start(f32[8,8,1]{2,1,0:T(8,128)} %get-tuple-element.379) | copy-start | bytes 772
  77.6 27.0 %copy-start.25 = (f32[8,8,1]{2,1,0:T(8,128)S(1)}, f32[8,8,1]{2,1,0:T(8,128)}, u32[]{:S(2)}) copy-start(f32[8,8,1]{2,1,0:T(8,128)} %get-tuple-element.380) | copy-start | bytes 772
  77.6 27.0 %copy-start.26 = (f32[8,8,1]{2,1,0:T(8,128)S(1)}, f32[8,8,1]{2,1,0:T(8,128)}, u32[]{:S(2)}) copy-start(f32[8,8,1]{2,1,0:T(8,128)} %get-tuple-element.381) | copy-start | bytes 772
  77.6 27.0 %copy-start.27 = (f32[8,8,1]{2,1,0:T(8,128)S(1)}, f32[8,8,1]{2,1,0:T(8,128)}, u32[]{:S(2)}) copy-start(f32[8,8,1]{2,1,0:T(8,128)} %get-tuple-element.382) | copy-start | bytes 772
  77.6 27.0 %copy-start.28 = (f32[8,8,1]{2,1,0:T(8,128)S(1)}, f32[8,8,1]{2,1,0:T(8,128)}, u32[]{:S(2)}) copy-start(f32[8,8,1]{2,1,0:T(8,128)} %get-tuple-element.383) | copy-start | bytes 772
  77.6 27.0 %copy-start.29 = (f32[8,8,1]{2,1,0:T(8,128)S(1)}, f32[8,8,1]{2,1,0:T(8,128)}, u32[]{:S(2)}) copy-start(f32[8,8,1]{2,1,0:T(8,128)} %get-tuple-element.384) | copy-start | bytes 772
  77.6 27.0 %copy-start.30 = (f32[8,8,1]{2,1,0:T(8,128)S(1)}, f32[8,8,1]{2,1,0:T(8,128)}, u32[]{:S(2)}) copy-start(f32[8,8,1]{2,1,0:T(8,128)} %get-tuple-element.385) | copy-start | bytes 772
  83.8 29.9 %copy-start.98 = (f32[8,128]{1,0:T(8,128)S(1)}, f32[8,128]{1,0:T(8,128)}, u32[]{:S(2)}) copy-start(f32[8,128]{1,0:T(8,128)} %get-tuple-element.142) | copy-start | bytes 12292
  97.4 38.7 %copy-start.15 = (f32[1,16,16,64]{3,2,1,0:T(8,128)}, f32[1,16,16,64]{3,2,1,0:T(8,128)S(1)}, u32[]{:S(2)}) copy-start(f32[1,16,16,64]{3,2,1,0:T(8,128)S(1)} %get-tuple-element.509) | copy-start | bytes 196612
  107.3 77.3 %collective-permute-start.1 = (f32[9,8,2,128]{3,2,1,0:T(2,128)}, f32[9,8,2,128]{3,2,1,0:T(2,128)S(1)}, u32[]{:S(2)}, u32[]{:S(2)}) collective-permute-start(f32[9,8,2,128]{3,2,1,0:T(2,128)} %get-tuple-element.204), channel_id=1, source_target_pairs={{16,0},{32,16},{48,32},{64,48},{80,64},{96,80},{112,96},{128,112},... | collective-permute-start | bytes 221192 | tf_op jit(solution)/shard_map/ppermute | solution.py:26
  114.4 4.4 %collective-permute-start.12 = (f32[10,1]{1,0:T(8,128)S(1)}, f32[10,1]{1,0:T(8,128)S(1)}, u32[]{:S(2)}, u32[]{:S(2)}) collective-permute-start(f32[10,1]{1,0:T(8,128)S(1)} %get-tuple-element.484), channel_id=1, source_target_pairs={{0,4},{4,8},{8,12},{1,5},{5,9},{9,13},{2,6},{6,10},{10,14},{3,7},{... | collective-permute-start | bytes 128 | tf_op jit(solution)/shard_map/ppermute | solution.py:25
  118.8 4.4 %collective-permute-start.13 = (f32[10,1]{1,0:T(8,128)S(1)}, f32[10,1]{1,0:T(8,128)S(1)}, u32[]{:S(2)}, u32[]{:S(2)}) collective-permute-start(f32[10,1]{1,0:T(8,128)S(1)} %get-tuple-element.485), channel_id=1, source_target_pairs={{4,0},{8,4},{12,8},{5,1},{9,5},{13,9},{6,2},{10,6},{14,10},{7,3},{... | collective-permute-start | bytes 128 | tf_op jit(solution)/shard_map/ppermute | solution.py:26
  137.6 7.6 %collective-permute-start.8 = (f32[3,16,20,2]{2,1,3,0:T(8,128)}, f32[3,16,20,2]{2,1,3,0:T(8,128)S(1)}, u32[]{:S(2)}, u32[]{:S(2)}) collective-permute-start(f32[3,16,20,2]{2,1,3,0:T(8,128)} %copy.1199), channel_id=1, source_target_pairs={{0,1},{1,2},{2,3},{3,4},{4,5},{5,6},{6,7},{7,8},{8,9},{9,10},{10,1... | collective-permute-start | bytes 23048 | tf_op jit(solution)/shard_map/ppermute | solution.py:25
  142.3 5.4 %collective-permute-start.9 = (f32[3,16,20,2]{2,1,3,0:T(8,128)S(1)}, f32[3,16,20,2]{2,1,3,0:T(8,128)S(1)}, u32[]{:S(2)}, u32[]{:S(2)}) collective-permute-start(f32[3,16,20,2]{2,1,3,0:T(8,128)S(1)} %copy.1200), channel_id=1, source_target_pairs={{1,0},{2,1},{3,2},{4,3},{5,4},{6,5},{7,6},{8,7},{9,8},{10,9},{11,1... | collective-permute-start | bytes 23048 | tf_op jit(solution)/shard_map/ppermute | solution.py:26
  185.5 8.5 %collective-permute-start.2 = (f32[9,8,12,2]{2,1,3,0:T(8,128)S(1)}, f32[9,8,12,2]{2,1,3,0:T(8,128)S(1)}, u32[]{:S(2)}, u32[]{:S(2)}) collective-permute-start(f32[9,8,12,2]{2,1,3,0:T(8,128)S(1)} %copy.917), channel_id=1, source_target_pairs={{0,4},{4,8},{8,12},{1,5},{5,9},{9,13},{2,6},{6,10},{10,14},{3,7},{... | collective-permute-start | bytes 20744 | tf_op jit(solution)/shard_map/ppermute | solution.py:25
  189.6 5.1 %collective-permute-start.3 = (f32[9,8,12,2]{2,1,3,0:T(8,128)S(1)}, f32[9,8,12,2]{2,1,3,0:T(8,128)S(1)}, u32[]{:S(2)}, u32[]{:S(2)}) collective-permute-start(f32[9,8,12,2]{2,1,3,0:T(8,128)S(1)} %copy.918), channel_id=1, source_target_pairs={{4,0},{8,4},{12,8},{5,1},{9,5},{13,9},{6,2},{10,6},{14,10},{7,3},{... | collective-permute-start | bytes 20744 | tf_op jit(solution)/shard_map/ppermute | solution.py:26
  196.5 9.5 %collective-permute-start.4 = (f32[9,2,12,132]{3,2,1,0:T(8,128)S(1)}, f32[9,2,12,132]{3,2,1,0:T(8,128)S(1)}, u32[]{:S(2)}, u32[]{:S(2)}) collective-permute-start(f32[9,2,12,132]{3,2,1,0:T(8,128)S(1)} %get-tuple-element.112), channel_id=1, source_target_pairs={{0,1},{1,2},{2,3},{4,5},{5,6},{6,7},{8,9},{9,10},{10,11},{12,13},{... | collective-permute-start | bytes 342152 | tf_op jit(solution)/shard_map/ppermute | solution.py:25
  200.1 8.0 %collective-permute-start.5 = (f32[9,2,12,132]{3,2,1,0:T(8,128)S(1)}, f32[9,2,12,132]{3,2,1,0:T(8,128)S(1)}, u32[]{:S(2)}, u32[]{:S(2)}) collective-permute-start(f32[9,2,12,132]{3,2,1,0:T(8,128)S(1)} %get-tuple-element.113), channel_id=1, source_target_pairs={{1,0},{2,1},{3,2},{5,4},{6,5},{7,6},{9,8},{10,9},{11,10},{13,12},{... | collective-permute-start | bytes 342152 | tf_op jit(solution)/shard_map/ppermute | solution.py:26
  (183 other events, 508.3 us)
where the time goes:
time: 217 us; the launch traced here: 215 us
  local copies, waits for them, and re-layouts  73.6 us (34%)
  other arithmetic  57.8 us (27%)
  starting transfers between devices  49.1 us (23%)
  blocking collectives  18 us (8%)
  waiting for transfers between devices  8.12 us (4%)
  between operations  5.43 us (3%)
  matrix products  2.93 us (1%)
    add x45, other arithmetic, closure(): running = running + weight * take_slab(field, col_index, 1, dimension)  25.7 us
    ppermute x7, starting transfers between devices, with_halo(): after = lax.ppermute(leading, axis, down)  25.3 us
    ppermute x7, starting transfers between devices, with_halo(): before = lax.ppermute(last, axis, up)  23.8 us
    mul x20, local copies, waits for them, and re-layouts, closure(): weight * take_slab(field, extent - 1 - col_index, 1, dimension)  19.8 us
    sub x15, local copies, waits for them, and re-layouts, closure(): running - weight * take_slab(field, extent - 1 - col_index, 1, dimension)  14.3 us
    unnamed x454, local copies, waits for them, and re-layouts  11.9 us
    psum x1, blocking collectives, broadcast(): return lax.psum(block, axis)  11.3 us
    mul x28, local copies, waits for them, and re-layouts, closure(): running = running + weight * take_slab(field, col_index, 1, dimension)  9.14 us
  transfers between devices with their start and end apart: 14, of which 5 were waited for; matrix products, arithmetic and copies ran while one was open for 56% of the time, Pallas kernels for 0%

commit v1 on v0

v1 whole, which is shorter than its diff:
```python
import functools

import jax
import jax.numpy as jnp
from jax import lax
from jax.experimental import pallas as pl
from jax.experimental.pallas import tpu as pltpu
from jax.sharding import PartitionSpec as P

closure_rows = (
    (-24.0 / 17.0, 59.0 / 34.0, -4.0 / 17.0, -3.0 / 34.0, 0.0, 0.0),
    (-0.5, 0.0, 0.5, 0.0, 0.0, 0.0),
    (4.0 / 43.0, -59.0 / 86.0, 0.0, 59.0 / 86.0, -4.0 / 43.0, 0.0),
    (3.0 / 98.0, 0.0, -59.0 / 98.0, 0.0, 32.0 / 49.0, -4.0 / 49.0),
)
inner_row = {-2: 1.0 / 12.0, -1: -8.0 / 12.0, 1: 8.0 / 12.0, 2: -1.0 / 12.0}
inv_norm = 48.0 / 17.0
step_size = 0.25
section_weight = 0.1496590219993
gravity = 0.4

MESH = pl.DeviceIdType.MESH
F32 = jnp.float32
HIGHEST = lax.Precision.HIGHEST
REACH = range(-3, 4)

x_fields = (0, 1, 2, 3, 7, 8)
y_fields = (0, 1, 2, 4, 6, 8)
z_fields = (0, 1, 2, 5, 6, 7)


def low_weight(k, d):
    return closure_rows[k][k + d] if 0 <= k + d < 6 else 0.0


def high_weight(k, d):
    return -closure_rows[k][k - d] if 0 <= k - d < 6 else 0.0


def weights(pos, n, first, last, closed):
    at_low = pos + jnp.where(first, 0, 4096)
    at_high = (n - 1) - pos + jnp.where(last, 0, 4096)
    table = {}
    for d in REACH:
        w = jnp.full(pos.shape, inner_row.get(d, 0.0), F32)
        if closed and d < 0:
            w = jnp.where(pos + d >= 0, w, 0.0)
        if closed and d > 0:
            w = jnp.where(pos + d < n, w, 0.0)
        for k in range(4):
            w = jnp.where(at_low == k, low_weight(k, d), w)
            w = jnp.where(at_high == k, high_weight(k, d), w)
        table[d] = w
    return table


def level_weights(level, n, first, last):
    table = {}
    for d in REACH:
        w = inner_row.get(d, 0.0)
        if level < 4 and first is not False:
            c = low_weight(level, d)
            w = c if first is True else (jnp.where(first, c, w) if c != w else w)
        elif level >= n - 4 and last is not False:
            c = high_weight(n - 1 - level, d)
            w = c if last is True else (jnp.where(last, c, w) if c != w else w)
        if not (isinstance(w, float) and w == 0.0):
            table[d] = w
    return table


def total(terms):
    out = None
    for term in terms:
        out = term if out is None else out + term
    return out


def roll_lanes(x, shift):
    return pltpu.roll(x, shift % 128, x.ndim - 1)


def rim_from_sides(left, right, lane, first, last):
    s = lax.rem(lane, 4)
    twelfth = 1.0 / 12.0
    from_left = jnp.where(first, 0.0, twelfth)
    from_right = jnp.where(last, 0.0, twelfth)
    one_left = jnp.where(s >= 2, from_left, 0.0)
    eight_left = jnp.where(s == 2, -8.0 * from_left, 0.0)
    one_right = jnp.where(s < 2, -from_right, 0.0)
    eight_right = jnp.where(s == 1, 8.0 * from_right, 0.0)
    return (
        one_left * roll_lanes(left, 2)
        + eight_left * roll_lanes(left, 1)
        + one_right * roll_lanes(right, -2)
        + eight_right * roll_lanes(right, -1)
    )


def section_kernel(
    sizes,
    solid, material, ocean, medium, off_x, off_y,
    s_next, s_rate, o_next, o_rate,
    sb, mb, ob, ov, med, ox, oy,
    z_low, z_high, plane, bed_part,
    ys_out, ys_left, ys_right, yo_out, yo_left, yo_right, coarse_out,
    dys, dyo, dzs, txs, opre, cat,
    local_sem, send_sem, recv_sem,
):
    nx, ny, nz = sizes
    gx, gy, gz = lax.axis_index("gx"), lax.axis_index("gy"), lax.axis_index("gz")
    up_x, down_x = lax.rem(gx + 1, nx), lax.rem(gx + nx - 1, nx)
    up_y, down_y = lax.rem(gy + 1, ny), lax.rem(gy + ny - 1, ny)
    x_first, x_last = gx == 0, gx == nx - 1
    y_first, y_last = gy == 0, gy == ny - 1
    z_first, z_last = gz == 0, gz == nz - 1
    right = (gx, jnp.where(z_last, up_y, gy), jnp.where(z_last, 0, gz + 1))
    left = (gx, jnp.where(z_first, down_y, gy), jnp.where(z_first, nz - 1, gz - 1))
    xs = {-1: down_x, 0: gx, 1: up_x}

    barrier = pltpu.get_barrier_semaphore()

    def greet(x, y, z):
        pl.semaphore_signal(barrier, inc=1, device_id=(x, y, z), device_id_type=MESH)

    greet(up_x, gy, gz)
    greet(down_x, gy, gz)
    greet(gx, up_y, gz)
    greet(gx, down_y, gz)
    greet(*right)
    greet(*left)

    @pl.when(z_first)
    def _():
        for e in (-1, 1):
            greet(xs[e], down_y, 0)
        for k in range(2, nz):
            greet(gx, gy, k)

    @pl.when(gz > 0)
    def _():
        for e in (-1, 1):
            greet(xs[e], gy, 0)

    @pl.when(gz > 1)
    def _():
        greet(gx, gy, 0)

    @pl.when(z_last)
    def _():
        for e in (-1, 1):
            greet(xs[e], up_y, 0)

    loads = [
        pltpu.make_async_copy(src, dst, local_sem.at[i])
        for i, (src, dst) in enumerate(
            (
                (solid, sb.at[:, :, 8:16]),
                (ocean.at[0:2], ob.at[:, :, 8:24]),
                (ocean.at[2:4], ov),
                (material, mb),
                (medium, med),
                (off_x, ox),
                (off_y, oy),
            )
        )
    ]
    for load in loads:
        load.start()

    @pl.when(z_first)
    def _():
        z_low[...] = jnp.zeros_like(z_low)

    @pl.when(z_last)
    def _():
        z_high[...] = jnp.zeros_like(z_high)

    @pl.when(z_first)
    def _():
        pl.semaphore_wait(barrier, 6 + (nz - 2) + 2 * (nz - 1) + 4)

    @pl.when(gz == 1)
    def _():
        pl.semaphore_wait(barrier, 6)

    @pl.when(gz > 1)
    def _():
        pl.semaphore_wait(barrier, 7)

    counter = iter(range(64))

    def remote(src, dst, recv, device):
        return pltpu.make_async_remote_copy(
            src_ref=src, dst_ref=dst, send_sem=send_sem.at[next(counter)], recv_sem=recv_sem.at[recv],
            device_id=device, device_id_type=MESH,
        )

    x_copies = []
    for i, (a, b) in enumerate(((0, 4), (7, 9))):
        x_copies.append(remote(solid.at[a:b, :, 6:8], sb.at[a:b, :, 6:8], 2 * i, (up_x, gy, gz)))
        x_copies.append(remote(solid.at[a:b, :, 0:2], sb.at[a:b, :, 16:18], 2 * i + 1, (down_x, gy, gz)))
    x_copies.append(remote(ocean.at[0:2, :, 14:16], ob.at[:, :, 6:8], 4, (up_x, gy, gz)))
    x_copies.append(remote(ocean.at[0:2, :, 0:2], ob.at[:, :, 24:26], 5, (down_x, gy, gz)))
    for copy in x_copies:
        copy.start()

    z_up = [
        remote(solid.at[a : a + 3, 6:8], z_low.at[b : b + 3], 6 + i, (gx, gy, gz + 1))
        for i, (a, b) in enumerate(((0, 0), (5, 3)))
    ]
    z_down = [
        remote(solid.at[a : a + 3, 0:2], z_high.at[b : b + 3], 8 + i, (gx, gy, gz - 1))
        for i, (a, b) in enumerate(((0, 0), (5, 3)))
    ]

    @pl.when(gz < nz - 1)
    def _():
        for copy in z_up:
            copy.start()

    @pl.when(gz > 0)
    def _():
        for copy in z_down:
            copy.start()

    tile = solid.at[2, 0]
    plane_copies = []
    for e in (-1, 0, 1):
        x = xs[-e]
        for k in range(nz):
            if e != 0 or k != 0:
                plane_copies.append(remote(tile, plane.at[0, e + 1], 10 + e + 1, (x, gy, k)))
        plane_copies.append(remote(tile, plane.at[1, e + 1], 13 + e + 1, (x, up_y, 0)))
        plane_copies.append(remote(tile, plane.at[1, e + 1], 13 + e + 1, (x, down_y, nz - 1)))
    own_plane = pltpu.make_async_copy(tile, plane.at[0, 1], local_sem.at[7])

    @pl.when(z_first)
    def _():
        own_plane.start()
        for copy in plane_copies:
            copy.start()

    lane = lax.broadcasted_iota(jnp.int32, (8, 128), 1)

    loads[0].wait()
    for half, fields in enumerate((y_fields[:4], y_fields[4:])):
        packed = jnp.zeros((8, 128), F32)
        for i, f in enumerate(fields):
            for z in range(8):
                k = 8 * i + z
                packed = jnp.where(lane // 4 == k, roll_lanes(sb[f, z, 8:16, :], 4 * k + 2), packed)
        ys_out[half] = packed
    ys_copies = [
        remote(ys_out, ys_left, 16, (gx, up_y, gz)),
        remote(ys_out, ys_right, 17, (gx, down_y, gz)),
    ]
    for copy in ys_copies:
        copy.start()

    loads[1].wait()
    loads[2].wait()
    half_lane = lax.rem(lane, 64)
    for i in range(2):
        packed = jnp.zeros((8, 128), F32)
        for d in range(16):
            if i == 0:
                both = jnp.concatenate([ob[0, d, 8:16, :], ob[0, d, 16:24, :]], axis=1)
            else:
                both = jnp.concatenate([ov[0, d, 0:8, :], ov[0, d, 8:16, :]], axis=1)
            cat[i, d] = both
            packed = jnp.where(half_lane // 4 == d, roll_lanes(both, 4 * d + 2), packed)
        yo_out[i] = packed
    yo_copies = [remote(yo_out, yo_left, 18, right), remote(yo_out, yo_right, 19, left)]
    for copy in yo_copies:
        copy.start()

    row = lax.broadcasted_iota(jnp.int32, (8, 16), 0)
    col = lax.broadcasted_iota(jnp.int32, (8, 16), 1)
    pair = jnp.where(col // 2 == row, 0.5, 0.0)
    fine = lax.broadcasted_iota(jnp.int32, (64, 128), 0)
    out_lane = lax.broadcasted_iota(jnp.int32, (64, 128), 1)
    place = jnp.where(out_lane == 32 * gz + fine // 2, 0.5, 0.0)
    coarse = jnp.dot(pair, ob[0, 15, 8:24, :], precision=HIGHEST, preferred_element_type=F32)
    coarse = jnp.dot(coarse, place, precision=HIGHEST, preferred_element_type=F32)
    coarse_out[...] = coarse
    coarse_copies = [remote(coarse_out, bed_part.at[k], 20 + k, (gx, gy, 0)) for k in range(1, nz)]
    for k in range(1, nz):

        @pl.when(gz == k)
        def _(k=k):
            coarse_copies[k - 1].start()

    wy = weights(lane, 128, y_first, y_last, True)
    for i, f in enumerate(y_fields):
        own = sb[f, :, 8:16, :]
        dys[i] = total(wy[d] * (roll_lanes(own, -d) if d else own) for d in REACH)
    wo = weights(half_lane, 64, jnp.logical_and(y_first, z_first), jnp.logical_and(y_last, z_last), True)
    for i in range(2):
        for d0 in range(0, 16, 8):
            own = cat[i, d0 : d0 + 8]
            dyo[i, d0 : d0 + 8] = total(wo[d] * (roll_lanes(own, -d) if d else own) for d in REACH)
    sub = lax.broadcasted_iota(jnp.int32, (8, 128), 0)
    wx = weights(sub, 8, x_first, x_last, False)
    for i, f in enumerate(x_fields):
        own = sb[f, :, 8:16, :]
        txs[i] = wx[0] * own + wx[3] * pltpu.roll(own, 5, 1) + wx[-3] * pltpu.roll(own, 3, 1)

    for copy in ys_copies:
        copy.wait_recv()
    at_edge = jnp.logical_or(lane < 2, lane >= 126)
    for half, fields in enumerate((y_fields[:4], y_fields[4:])):
        rim = rim_from_sides(ys_left[half], ys_right[half], lane, y_first, y_last)
        for i in range(len(fields)):
            for z in range(8):
                k = 8 * i + z
                dys[4 * half + i, z] += jnp.where(at_edge, roll_lanes(rim, -4 * k - 2), 0.0)
    for copy in yo_copies:
        copy.wait_recv()
    at_half_edge = jnp.logical_or(half_lane < 2, half_lane >= 62)
    for i in range(2):
        rim = rim_from_sides(
            roll_lanes(yo_left[i], 64), roll_lanes(yo_right[i], 64), lane,
            jnp.logical_and(y_first, z_first), jnp.logical_and(y_last, z_last),
        )
        for d in range(16):
            dyo[i, d] += jnp.where(at_half_edge, roll_lanes(rim, -4 * d - 2), 0.0)

    loads[3].wait()

    @pl.when(gz > 0)
    def _():
        for copy in z_up:
            copy.wait_recv()

    @pl.when(gz < nz - 1)
    def _():
        for copy in z_down:
            copy.wait_recv()

    for i, f in enumerate(z_fields):
        def level(z, i=i, f=f):
            if z < 0:
                return z_low[i, z + 2]
            if z >= 8:
                return z_high[i, z - 8]
            return sb[f, z, 8:16, :]

        for z in range(8):
            table = level_weights(z, 8, z_first, z_last)
            dzs[i, z] = mb[3, z] * total(w * level(z + d) for d, w in table.items() if -2 <= z + d < 10)

    @pl.when(z_first)
    def _():
        for k in range(1, nz):
            pltpu.make_async_remote_copy(
                src_ref=coarse_out, dst_ref=bed_part.at[k], send_sem=send_sem.at[63], recv_sem=recv_sem.at[20 + k],
                device_id=(gx, up_y, gz), device_id_type=MESH,
            ).wait_recv()
        scale = inv_norm * mb[3, 0]
        bed_pressure = coarse_out[...] + total(bed_part[k] for k in range(1, nz))
        dzs[5, 0] += scale * sb[7, 0, 8:16, :]
        dzs[4, 0] += scale * sb[6, 0, 8:16, :]
        dzs[3, 0] += scale * (sb[5, 0, 8:16, :] + bed_pressure)

    loads[5].wait()
    loads[6].wait()

    def plane_wait(s, e):
        pltpu.make_async_remote_copy(
            src_ref=tile, dst_ref=plane.at[s, e + 1], send_sem=send_sem.at[63], recv_sem=recv_sem.at[10 + 3 * s + e + 1],
            device_id=(gx, up_y, gz), device_id_type=MESH,
        ).wait_recv()

    plane_wait(0, -1)
    plane_wait(0, 1)

    @pl.when(z_first)
    def _():
        own_plane.wait()
        for e in (-1, 0, 1):
            plane_wait(1, e)
            plane[0, e + 1] = jnp.where(lane == 127, plane[1, e + 1], plane[0, e + 1])

    @pl.when(gz > 0)
    def _():
        plane_wait(0, 0)

    @pl.when(z_last)
    def _():
        for e in (-1, 0, 1):
            plane_wait(1, e)
            plane[0, e + 1] = jnp.where(lane == 0, plane[1, e + 1], plane[0, e + 1])

    window = plane[0].reshape(24, 128)
    fine_x = lax.broadcasted_iota(jnp.int32, (24, 16), 1)
    coarse_x = lax.broadcasted_iota(jnp.int32, (24, 16), 0) + (8 * gx - 8)
    near_x = 8 * gx + fine_x // 2
    far_x = jnp.clip(near_x + ox[...], 0, 8 * nx - 1)
    blend_x = jnp.where(coarse_x == near_x, 0.75, 0.0) + jnp.where(coarse_x == far_x, 0.25, 0.0)
    fine_y = lax.broadcasted_iota(jnp.int32, (128, 64), 1)
    coarse_y = lax.broadcasted_iota(jnp.int32, (128, 64), 0)
    near_y = 128 * gy + 32 * gz + fine_y // 2
    far_y = jnp.clip(near_y + oy[...], 0, 128 * ny - 1)
    blend_y = jnp.where(coarse_y == lax.rem(near_y, 128), 0.75, 0.0)
    blend_y = blend_y + jnp.where(coarse_y == lax.rem(far_y, 128), 0.25, 0.0)
    bed_speed = lax.dot_general(
        blend_x, window, (((0,), (0,)), ((), ())), precision=HIGHEST, preferred_element_type=F32
    )
    bed_speed = jnp.dot(bed_speed, blend_y, precision=HIGHEST, preferred_element_type=F32)

    loads[4].wait()

    def unfold(i, d):
        both = dyo[i, d]
        return jnp.concatenate([both[:, 0:64], both[:, 64:128]], axis=0)

    for d in range(16):
        bulk = jnp.full((16, 64), med[0, d], F32)
        light = jnp.full((16, 64), med[1, d], F32)
        pressure, flow_v, flow_w = ob[0, d, 8:24, :], ov[0, d], ov[1, d]
        table = level_weights(d, 16, True, True)
        dz_w = total(w * ov[1, d + k] for k, w in table.items())
        dz_p = total(w * ob[0, d + k, 8:24, :] for k, w in table.items())
        part = -bulk * (2.0 * unfold(1, d) + dz_w) + gravity * flow_w / light
        if d == 15:
            part = part + inv_norm * bulk * (flow_w - bed_speed)
        opre[d] = step_size * part
        rate_v = (-2.0 * step_size) * light * unfold(0, d)
        rate_w = -light * dz_p
        if d == 0:
            rate_w = rate_w - inv_norm * light * pressure
        rate_w = step_size * rate_w
        o_rate[2, d] = rate_v
        o_rate[3, d] = rate_w
        o_next[2, d] = flow_v + section_weight * rate_v
        o_next[3, d] = flow_w + section_weight * rate_w

    for copy in x_copies:
        copy.wait_recv()

    def dx(i, f, z):
        out = txs[i, z]
        for d in (-2, -1, 1, 2):
            out = out + wx[d] * sb[f, z, 8 + d : 16 + d, :]
        return out

    for z in range(8):
        own = [sb[f, z, 8:16, :] for f in range(9)]
        b, lam, mu = step_size * mb[0, z], step_size * mb[1, z], step_size * mb[2, z]
        d_x = {f: dx(i, f, z) for i, f in enumerate(x_fields)}
        d_y = {f: dys[i, z] for i, f in enumerate(y_fields)}
        d_z = {f: dzs[i, z] for i, f in enumerate(z_fields)}
        dilation = lam * (d_x[0] + d_y[1] + d_z[2])
        mu2 = 2.0 * mu
        rates = [
            b * (d_x[3] + d_y[8] + d_z[7]),
            b * (d_x[8] + d_y[4] + d_z[6]),
            b * (d_x[7] + d_y[6] + d_z[5]),
            dilation + mu2 * d_x[0],
            dilation + mu2 * d_y[1],
            dilation + mu2 * d_z[2],
            mu * (d_z[1] + d_y[2]),
            mu * (d_z[0] + d_x[2]),
            mu * (d_y[0] + d_x[1]),
        ]
        for f in range(9):
            s_rate[f, z] = rates[f]
            s_next[f, z] = own[f] + section_weight * rates[f]

    pos = lax.broadcasted_iota(jnp.int32, (16, 64), 0)
    wp = weights(pos, 16, x_first, x_last, False)
    far_up, far_down = wp[3] != 0.0, wp[-3] != 0.0

    def dx_ocean(i, d):
        out = total(wp[k] * ob[i, d, 8 + k : 24 + k, :] for k in range(-2, 3))
        out = out + wp[3] * jnp.where(far_up, ob[i, d, 11:27, :], 0.0)
        return out + wp[-3] * jnp.where(far_down, ob[i, d, 5:21, :], 0.0)

    for d in range(16):
        bulk = jnp.full((16, 64), (-2.0 * step_size) * med[0, d], F32)
        light = jnp.full((16, 64), (-2.0 * step_size) * med[1, d], F32)
        rate_p = opre[d] + bulk * dx_ocean(1, d)
        rate_u = light * dx_ocean(0, d)
        o_rate[0, d] = rate_p
        o_rate[1, d] = rate_u
        o_next[0, d] = ob[0, d, 8:24, :] + section_weight * rate_p
        o_next[1, d] = ob[1, d, 8:24, :] + section_weight * rate_u

    for copy in x_copies + ys_copies + yo_copies:
        copy.wait_send()

    @pl.when(gz < nz - 1)
    def _():
        for copy in z_up:
            copy.wait_send()

    @pl.when(gz > 0)
    def _():
        for copy in z_down:
            copy.wait_send()

    @pl.when(z_first)
    def _():
        for copy in plane_copies:
            copy.wait_send()

    for k in range(1, nz):

        @pl.when(gz == k)
        def _(k=k):
            coarse_copies[k - 1].wait_send()


def write_kernel(*refs):
    count = (len(refs) - 1) // 2
    sem = refs[-1]
    copies = [pltpu.make_async_copy(refs[i], refs[count + i], sem.at[i]) for i in range(count)]
    for copy in copies:
        copy.start()
    for copy in copies:
        copy.wait()


def body(sizes, solid_state, material, ocean_state, ocean_medium, offset_x, offset_y):
    outs = (solid_state.shape, solid_state.shape, ocean_state.shape, ocean_state.shape)
    v = lambda *shape: pltpu.VMEM(shape, F32)
    held = pl.pallas_call(
        functools.partial(section_kernel, sizes),
        out_shape=[pltpu.VMEM(shape, F32) for shape in outs],
        in_specs=[pl.BlockSpec(memory_space=pltpu.HBM)] * 6,
        out_specs=[pl.BlockSpec(memory_space=pltpu.VMEM)] * 4,
        scratch_shapes=[
            v(9, 8, 24, 128), v(4, 8, 8, 128), v(2, 16, 32, 64), v(2, 16, 16, 64),
            pltpu.SMEM((2, 16), F32), pltpu.VMEM((1, 16), jnp.int32), pltpu.VMEM((1, 64), jnp.int32),
            v(6, 2, 8, 128), v(6, 2, 8, 128), v(2, 3, 8, 128), v(4, 8, 128),
            v(2, 8, 128), v(2, 8, 128), v(2, 8, 128), v(2, 8, 128), v(2, 8, 128), v(2, 8, 128), v(8, 128),
            v(6, 8, 8, 128), v(2, 16, 8, 128), v(6, 8, 8, 128), v(6, 8, 8, 128), v(16, 16, 64), v(2, 16, 8, 128),
            pltpu.SemaphoreType.DMA((8,)), pltpu.SemaphoreType.DMA((64,)), pltpu.SemaphoreType.DMA((24,)),
        ],
        compiler_params=pltpu.CompilerParams(
            vmem_limit_bytes=16 * 2**20, collective_id=0, has_side_effects=True
        ),
        name="section",
    )(solid_state, material, ocean_state, ocean_medium, offset_x.reshape(1, -1), offset_y.reshape(1, -1))
    return pl.pallas_call(
        write_kernel,
        out_shape=[jax.ShapeDtypeStruct(shape, F32) for shape in outs],
        in_specs=[pl.BlockSpec(memory_space=pltpu.VMEM)] * 4,
        out_specs=[pl.BlockSpec(memory_space=pl.ANY)] * 4,
        scratch_shapes=[pltpu.SemaphoreType.DMA((4,))],
        compiler_params=pltpu.CompilerParams(vmem_limit_bytes=4 * 2**20),
        name="write_out",
    )(*held)


def solution(mesh):
    sizes = (mesh.shape["gx"], mesh.shape["gy"], mesh.shape["gz"])
    solid = P(None, "gz", "gx", "gy")
    ocean = P(None, None, "gx", ("gy", "gz"))
    return jax.shard_map(
        functools.partial(body, sizes),
        mesh=mesh,
        in_specs=(solid, solid, ocean, P(), P("gx"), P(("gy", "gz"))),
        out_specs=(solid, solid, ocean, ocean),
        check_vma=False,
    )
```

time: 217 us -> 24.6 us (0.11)
  the two profiles are of different devices: /device:TPU:15 before, /device:TPU:1 now
where the time goes in v1:
time: 24.6 us; the launch traced here: 24.4 us
  Pallas kernels  20.1 us (82%)
  local copies, waits for them, and re-layouts  3.58 us (15%)
  between operations  0.67 us (3%)
    pallas_call x1, Pallas kernels, body(): pl.pallas_call(functools.partial(section_kernel, sizes), out_shape=[pltpu...  18.9 us
    unnamed x12, local copies, waits for them, and re-layouts  3.58 us
    pallas_call x1, Pallas kernels, body(): pl.pallas_call(write_kernel, out_shape=[jax.ShapeDtypeStruct(shape, F32)...  1.2 us

profile of v1, /device:TPU:1, one launch (start us, length us, event | category | flops | bytes accessed | tf_op | source)
XLA Modules:
  0.0 24.4 jit_solution(4240905543239184909)
XLA Ops:
  0.6 0.0 copy-start.5
  0.6 0.0 copy-start.3
  0.7 0.0 copy-start.4
  0.7 0.6 %copy-done.5 = s32[64]{0:T(128)S(1)} copy-done((s32[64]{0:T(128)S(1)}, s32[64]{0:T(128)}, u32[]{:S(2)}) %copy-start.5) | copy-done | bytes 280
  1.3 0.0 copy-done.3
  1.3 0.0 copy-done.4
  1.3 0.0 copy-start
  1.3 1.0 %copy-done = f32[4,16,16,64]{3,2,1,0:T(8,128)S(1)} copy-done((f32[4,16,16,64]{3,2,1,0:T(8,128)S(1)}, f32[4,16,16,64]{3,2,1,0:T(8,128)}, u32[]{:S(2)}) %copy-start) | copy-done | bytes 262168
  2.4 0.0 copy-start.1
  2.4 1.0 %copy-done.1 = f32[9,8,8,128]{3,2,1,0:T(8,128)S(1)} copy-done((f32[9,8,8,128]{3,2,1,0:T(8,128)S(1)}, f32[9,8,8,128]{3,2,1,0:T(8,128)}, u32[]{:S(2)}) %copy-start.1) | copy-done | bytes 294936
  3.3 0.0 copy-start.2
  3.3 0.9 %copy-done.2 = f32[4,8,8,128]{3,2,1,0:T(8,128)S(1)} copy-done((f32[4,8,8,128]{3,2,1,0:T(8,128)S(1)}, f32[4,8,8,128]{3,2,1,0:T(8,128)}, u32[]{:S(2)}) %copy-start.2) | copy-done | bytes 131096
  4.2 18.9 %section.1 = (f32[9,8,8,128]{3,2,1,0:T(8,128)S(1)}, f32[9,8,8,128]{3,2,1,0:T(8,128)S(1)}, f32[4,16,16,64]{3,2,1,0:T(8,128)S(1)}, f32[4,16,16,64]{3,2,1,0:T(8,128)S(1)}) custom-call(f32[9,8,8,128]{3,2,1,0:T(8,128)S(1)} %copy-done.1, f32[4,8,8,128]{3,2,1,0:T(8,128)S(1)} %copy-done.2, f32[4,16,16,64]{3,2,1,0:T(8,128)S(1)} %copy-done, f32[2,16]{1,0:T(2,128)S(1)} %copy-done.3, ...), custom_call_target="tpu_custom_call" | custom-call | tf_op jit(solution)/shard_map/section/pallas_call | solution.py:528
  23.2 1.2 %write_out.1 = (f32[9,8,8,128]{3,2,1,0:T(8,128)}, f32[9,8,8,128]{3,2,1,0:T(8,128)}, f32[4,16,16,64]{3,2,1,0:T(8,128)}, f32[4,16,16,64]{3,2,1,0:T(8,128)}) custom-call(f32[9,8,8,128]{3,2,1,0:T(8,128)S(1)} %get-tuple-element.8.refs_0_, f32[9,8,8,128]{3,2,1,0:T(8,128)S(1)} %get-tuple-element.9.refs_1_, f32[4,16,16,64]{3,2,1,0:T(8,128)S(1)} %get-tuple-element.10.refs_2_, ...), custom_call_target="tpu_custom_call" | custom-call | tf_op jit(solution)/shard_map/write_out/pallas_call | solution.py:546
Async XLA Ops:
  0.6 0.7 %copy-start.5 = (s32[64]{0:T(128)S(1)}, s32[64]{0:T(128)}, u32[]{:S(2)}) copy-start(s32[64]{0:T(128)} %param.11) | copy-start | bytes 772
  0.6 0.7 %copy-start.3 = (f32[2,16]{1,0:T(2,128)S(1)}, f32[2,16]{1,0:T(2,128)}, u32[]{:S(2)}) copy-start(f32[2,16]{1,0:T(2,128)} %medium.1) | copy-start | bytes 388
  0.7 0.7 %copy-start.4 = (s32[16]{0:T(128)S(1)}, s32[16]{0:T(128)}, u32[]{:S(2)}) copy-start(s32[16]{0:T(128)} %param.10) | copy-start | bytes 196
  1.3 1.0 %copy-start = (f32[4,16,16,64]{3,2,1,0:T(8,128)S(1)}, f32[4,16,16,64]{3,2,1,0:T(8,128)}, u32[]{:S(2)}) copy-start(f32[4,16,16,64]{3,2,1,0:T(8,128)} %ocean.1) | copy-start | bytes 786436
  2.4 1.0 %copy-start.1 = (f32[9,8,8,128]{3,2,1,0:T(8,128)S(1)}, f32[9,8,8,128]{3,2,1,0:T(8,128)}, u32[]{:S(2)}) copy-start(f32[9,8,8,128]{3,2,1,0:T(8,128)} %solid.1) | copy-start | bytes 884740
  3.3 0.9 %copy-start.2 = (f32[4,8,8,128]{3,2,1,0:T(8,128)S(1)}, f32[4,8,8,128]{3,2,1,0:T(8,128)}, u32[]{:S(2)}) copy-start(f32[4,8,8,128]{3,2,1,0:T(8,128)} %material.1) | copy-start | bytes 393220

commit v2 on v1

--- a/solution.py
+++ b/solution.py
@@ -95,6 +95,24 @@
         + one_right * roll_lanes(right, -2)
         + eight_right * roll_lanes(right, -1)
     )
+
+
+def when(pred, action):
+    @pl.when(pred)
+    def _():
+        action()
+
+
+def start(pred, *copies):
+    when(pred, lambda: [copy.start() for copy in copies] and None)
+
+
+def landed(pred, *copies):
+    when(pred, lambda: [copy.wait_recv() for copy in copies] and None)
+
+
+def sent(pred, *copies):
+    when(pred, lambda: [copy.wait_send() for copy in copies] and None)
 
 
 def section_kernel(
@@ -123,33 +141,26 @@
     def greet(x, y, z):
         pl.semaphore_signal(barrier, inc=1, device_id=(x, y, z), device_id_type=MESH)
 
-    greet(up_x, gy, gz)
-    greet(down_x, gy, gz)
-    greet(gx, up_y, gz)
-    greet(gx, down_y, gz)
-    greet(*right)
-    greet(*left)
-
-    @pl.when(z_first)
-    def _():
-        for e in (-1, 1):
-            greet(xs[e], down_y, 0)
-        for k in range(2, nz):
-            greet(gx, gy, k)
-
-    @pl.when(gz > 0)
-    def _():
-        for e in (-1, 1):
-            greet(xs[e], gy, 0)
-
-    @pl.when(gz > 1)
-    def _():
-        greet(gx, gy, 0)
-
-    @pl.when(z_last)
-    def _():
-        for e in (-1, 1):
-            greet(xs[e], up_y, 0)
+    x_down, x_up = gx > 0, gx < nx - 1
+    y_down, y_up = gy > 0, gy < ny - 1
+    z_down, z_up = gz > 0, gz < nz - 1
+    has_left, has_right = jnp.logical_or(y_down, z_down), jnp.logical_or(y_up, z_up)
+    both = jnp.logical_and
+    has = {-1: x_down, 1: x_up}
+
+    when(x_up, lambda: greet(up_x, gy, gz))
+    when(x_down, lambda: greet(down_x, gy, gz))
+    when(y_up, lambda: greet(gx, up_y, gz))
+    when(y_down, lambda: greet(gx, down_y, gz))
+    when(has_right, lambda: greet(*right))
+    when(has_left, lambda: greet(*left))
+    for k in range(2, nz):
+        when(z_first, lambda: greet(gx, gy, k))
+    when(gz > 1, lambda: greet(gx, gy, 0))
+    for e in (-1, 1):
+        when(both(has[e], z_down), lambda: greet(xs[e], gy, 0))
+        when(both(has[e], both(z_first, y_down)), lambda: greet(xs[e], down_y, 0))
+        when(both(has[e], both(z_last, y_up)), lambda: greet(xs[e], up_y, 0))
 
     loads = [
         pltpu.make_async_copy(src, dst, local_sem.at[i])
@@ -168,25 +179,26 @@
     for load in loads:
         load.start()
 
-    @pl.when(z_first)
-    def _():
-        z_low[...] = jnp.zeros_like(z_low)
-
-    @pl.when(z_last)
-    def _():
-        z_high[...] = jnp.zeros_like(z_high)
-
-    @pl.when(z_first)
-    def _():
-        pl.semaphore_wait(barrier, 6 + (nz - 2) + 2 * (nz - 1) + 4)
-
-    @pl.when(gz == 1)
-    def _():
-        pl.semaphore_wait(barrier, 6)
-
-    @pl.when(gz > 1)
-    def _():
-        pl.semaphore_wait(barrier, 7)
+    def clear(*places):
+        for ref in places:
+            ref[...] = jnp.zeros(ref.shape, F32)
+
+    when(z_first, lambda: clear(z_low))
+    when(z_last, lambda: clear(z_high))
+    when(x_first, lambda: clear(sb.at[:, :, 6:8], ob.at[:, :, 6:8], plane.at[:, 0]))
+    when(x_last, lambda: clear(sb.at[:, :, 16:18], ob.at[:, :, 24:26], plane.at[:, 2]))
+    when(y_first, lambda: clear(ys_left))
+    when(y_last, lambda: clear(ys_right))
+    when(jnp.logical_not(has_left), lambda: clear(yo_left, plane.at[1]))
+    when(jnp.logical_not(has_right), lambda: clear(yo_right, plane.at[1]))
+
+    def count(*preds):
+        return sum(jnp.where(p, 1, 0) for p in preds)
+
+    n_x, n_y = count(x_down, x_up), count(y_down, y_up)
+    n_side = count(has_left, has_right)
+    first_extra = (nz - 2) + n_x * (nz - 1 + n_y)
+    pl.semaphore_wait(barrier, n_x + n_y + n_side + jnp.where(z_first, first_extra, jnp.where(gz > 1, 1, 0)))
 
     counter = iter(range(64))
 
@@ -196,50 +208,39 @@
             device_id=device, device_id_type=MESH,
         )
 
-    x_copies = []
+    up_copies, down_copies = [], []
     for i, (a, b) in enumerate(((0, 4), (7, 9))):
-        x_copies.append(remote(solid.at[a:b, :, 6:8], sb.at[a:b, :, 6:8], 2 * i, (up_x, gy, gz)))
-        x_copies.append(remote(solid.at[a:b, :, 0:2], sb.at[a:b, :, 16:18], 2 * i + 1, (down_x, gy, gz)))
-    x_copies.append(remote(ocean.at[0:2, :, 14:16], ob.at[:, :, 6:8], 4, (up_x, gy, gz)))
-    x_copies.append(remote(ocean.at[0:2, :, 0:2], ob.at[:, :, 24:26], 5, (down_x, gy, gz)))
-    for copy in x_copies:
-        copy.start()
-
-    z_up = [
+        up_copies.append(remote(solid.at[a:b, :, 6:8], sb.at[a:b, :, 6:8], 2 * i, (up_x, gy, gz)))
+        down_copies.append(remote(solid.at[a:b, :, 0:2], sb.at[a:b, :, 16:18], 2 * i + 1, (down_x, gy, gz)))
+    up_copies.append(remote(ocean.at[0:2, :, 14:16], ob.at[:, :, 6:8], 4, (up_x, gy, gz)))
+    down_copies.append(remote(ocean.at[0:2, :, 0:2], ob.at[:, :, 24:26], 5, (down_x, gy, gz)))
+    start(x_up, *up_copies)
+    start(x_down, *down_copies)
+
+    z_up_copies = [
         remote(solid.at[a : a + 3, 6:8], z_low.at[b : b + 3], 6 + i, (gx, gy, gz + 1))
         for i, (a, b) in enumerate(((0, 0), (5, 3)))
     ]
-    z_down = [
+    z_down_copies = [
         remote(solid.at[a : a + 3, 0:2], z_high.at[b : b + 3], 8 + i, (gx, gy, gz - 1))
         for i, (a, b) in enumerate(((0, 0), (5, 3)))
     ]
-
-    @pl.when(gz < nz - 1)
-    def _():
-        for copy in z_up:
-            copy.start()
-
-    @pl.when(gz > 0)
-    def _():
-        for copy in z_down:
-            copy.start()
+    start(z_up, *z_up_copies)
+    start(z_down, *z_down_copies)
 
     tile = solid.at[2, 0]
     plane_copies = []
     for e in (-1, 0, 1):
         x = xs[-e]
-        for k in range(nz):
-            if e != 0 or k != 0:
-                plane_copies.append(remote(tile, plane.at[0, e + 1], 10 + e + 1, (x, gy, k)))
-        plane_copies.append(remote(tile, plane.at[1, e + 1], 13 + e + 1, (x, up_y, 0)))
-        plane_copies.append(remote(tile, plane.at[1, e + 1], 13 + e + 1, (x, down_y, nz - 1)))
+        there = z_first if e == 0 else both(z_first, has[-e])
+        mine = [remote(tile, plane.at[0, e + 1], 10 + e + 1, (x, gy, k)) for k in range(1 if e == 0 else 0, nz)]
+        plane_copies.append((there, mine))
+        plane_copies.append((both(there, y_up), [remote(tile, plane.at[1, e + 1], 13 + e + 1, (x, up_y, 0))]))
+        plane_copies.append((both(there, y_down), [remote(tile, plane.at[1, e + 1], 13 + e + 1, (x, down_y, nz - 1))]))
     own_plane = pltpu.make_async_copy(tile, plane.at[0, 1], local_sem.at[7])
-
-    @pl.when(z_first)
-    def _():
-        own_plane.start()
-        for copy in plane_copies:
-            copy.start()
+    when(z_first, own_plane.start)
+    for pred, copies in plane_copies:
+        start(pred, *copies)
 
     lane = lax.broadcasted_iota(jnp.int32, (8, 128), 1)
 
@@ -255,8 +256,8 @@
         remote(ys_out, ys_left, 16, (gx, up_y, gz)),
         remote(ys_out, ys_right, 17, (gx, down_y, gz)),
     ]
-    for copy in ys_copies:
-        copy.start()
+    start(y_up, ys_copies[0])
+    start(y_down, ys_copies[1])
 
     loads[1].wait()
     loads[2].wait()
@@ -265,15 +266,15 @@
         packed = jnp.zeros((8, 128), F32)
         for d in range(16):
             if i == 0:
-                both = jnp.concatenate([ob[0, d, 8:16, :], ob[0, d, 16:24, :]], axis=1)
+                folded = jnp.concatenate([ob[0, d, 8:16, :], ob[0, d, 16:24, :]], axis=1)
             else:
-                both = jnp.concatenate([ov[0, d, 0:8, :], ov[0, d, 8:16, :]], axis=1)
-            cat[i, d] = both
-            packed = jnp.where(half_lane // 4 == d, roll_lanes(both, 4 * d + 2), packed)
+                folded = jnp.concatenate([ov[0, d, 0:8, :], ov[0, d, 8:16, :]], axis=1)
+            cat[i, d] = folded
+            packed = jnp.where(half_lane // 4 == d, roll_lanes(folded, 4 * d + 2), packed)
         yo_out[i] = packed
     yo_copies = [remote(yo_out, yo_left, 18, right), remote(yo_out, yo_right, 19, left)]
-    for copy in yo_copies:
-        copy.start()
+    start(has_right, yo_copies[0])
+    start(has_left, yo_copies[1])
 
     row = lax.broadcasted_iota(jnp.int32, (8, 16), 0)
     col = lax.broadcasted_iota(jnp.int32, (8, 16), 1)
@@ -286,10 +287,7 @@
     coarse_out[...] = coarse
     coarse_copies = [remote(coarse_out, bed_part.at[k], 20 + k, (gx, gy, 0)) for k in range(1, nz)]
     for k in range(1, nz):
-
-        @pl.when(gz == k)
-        def _(k=k):
-            coarse_copies[k - 1].start()
+        start(gz == k, coarse_copies[k - 1])
 
     wy = weights(lane, 128, y_first, y_last, True)
     for i, f in enumerate(y_fields):
@@ -306,8 +304,8 @@
         own = sb[f, :, 8:16, :]
         txs[i] = wx[0] * own + wx[3] * pltpu.roll(own, 5, 1) + wx[-3] * pltpu.roll(own, 3, 1)
 
-    for copy in ys_copies:
-        copy.wait_recv()
+    landed(y_down, ys_copies[0])
+    landed(y_up, ys_copies[1])
     at_edge = jnp.logical_or(lane < 2, lane >= 126)
     for half, fields in enumerate((y_fields[:4], y_fields[4:])):
         rim = rim_from_sides(ys_left[half], ys_right[half], lane, y_first, y_last)
@@ -315,8 +313,8 @@
             for z in range(8):
                 k = 8 * i + z
                 dys[4 * half + i, z] += jnp.where(at_edge, roll_lanes(rim, -4 * k - 2), 0.0)
-    for copy in yo_copies:
-        copy.wait_recv()
+    landed(has_left, yo_copies[0])
+    landed(has_right, yo_copies[1])
     at_half_edge = jnp.logical_or(half_lane < 2, half_lane >= 62)
     for i in range(2):
         rim = rim_from_sides(
@@ -328,15 +326,8 @@
 
     loads[3].wait()
 
-    @pl.when(gz > 0)
-    def _():
-        for copy in z_up:
-            copy.wait_recv()
-
-    @pl.when(gz < nz - 1)
-    def _():
-        for copy in z_down:
-            copy.wait_recv()
+    landed(z_down, *z_up_copies)
+    landed(z_up, *z_down_copies)
 
     for i, f in enumerate(z_fields):
         def level(z, i=i, f=f):
@@ -372,25 +363,19 @@
             device_id=(gx, up_y, gz), device_id_type=MESH,
         ).wait_recv()
 
-    plane_wait(0, -1)
-    plane_wait(0, 1)
-
-    @pl.when(z_first)
-    def _():
-        own_plane.wait()
-        for e in (-1, 0, 1):
-            plane_wait(1, e)
-            plane[0, e + 1] = jnp.where(lane == 127, plane[1, e + 1], plane[0, e + 1])
-
-    @pl.when(gz > 0)
-    def _():
-        plane_wait(0, 0)
-
-    @pl.when(z_last)
-    def _():
-        for e in (-1, 0, 1):
-            plane_wait(1, e)
-            plane[0, e + 1] = jnp.where(lane == 0, plane[1, e + 1], plane[0, e + 1])
+    when(z_first, own_plane.wait)
+    when(z_down, lambda: plane_wait(0, 0))
+    for e in (-1, 1):
+        when(has[e], lambda: plane_wait(0, e))
+    for pred, at in ((both(z_first, y_down), 127), (both(z_last, y_up), 0)):
+        when(pred, lambda: plane_wait(1, 0))
+        for e in (-1, 1):
+            when(both(pred, has[e]), lambda: plane_wait(1, e))
+
+        @pl.when(pred)
+        def _(at=at):
+            for e in range(3):
+                plane[0, e] = jnp.where(lane == at, plane[1, e], plane[0, e])
 
     window = plane[0].reshape(24, 128)
     fine_x = lax.broadcasted_iota(jnp.int32, (24, 16), 1)
@@ -412,8 +397,8 @@
     loads[4].wait()
 
     def unfold(i, d):
-        both = dyo[i, d]
-        return jnp.concatenate([both[:, 0:64], both[:, 64:128]], axis=0)
+        folded = dyo[i, d]
+        return jnp.concatenate([folded[:, 0:64], folded[:, 64:128]], axis=0)
 
     for d in range(16):
         bulk = jnp.full((16, 64), med[0, d], F32)
@@ -436,8 +421,8 @@
         o_next[2, d] = flow_v + section_weight * rate_v
         o_next[3, d] = flow_w + section_weight * rate_w
 
-    for copy in x_copies:
-        copy.wait_recv()
+    landed(x_down, *up_copies)
+    landed(x_up, *down_copies)
 
     def dx(i, f, z):
         out = txs[i, z]
@@ -487,29 +472,18 @@
         o_next[0, d] = ob[0, d, 8:24, :] + section_weight * rate_p
         o_next[1, d] = ob[1, d, 8:24, :] + section_weight * rate_u
 
-    for copy in x_copies + ys_copies + yo_copies:
-        copy.wait_send()
-
-    @pl.when(gz < nz - 1)
-    def _():
-        for copy in z_up:
-            copy.wait_send()
-
-    @pl.when(gz > 0)
-    def _():
-        for copy in z_down:
-            copy.wait_send()
-
-    @pl.when(z_first)
-    def _():
-        for copy in plane_copies:
-            copy.wait_send()
-
+    sent(x_up, *up_copies)
+    sent(x_down, *down_copies)
+    sent(y_up, ys_copies[0])
+    sent(y_down, ys_copies[1])
+    sent(has_right, yo_copies[0])
+    sent(has_left, yo_copies[1])
+    sent(z_up, *z_up_copies)
+    sent(z_down, *z_down_copies)
+    for pred, copies in plane_copies:
+        sent(pred, *copies)
     for k in range(1, nz):
-
-        @pl.when(gz == k)
-        def _(k=k):
-            coarse_copies[k - 1].wait_send()
+        sent(gz == k, coarse_copies[k - 1])
 
 
 def write_kernel(*refs):
@@ -542,7 +516,10 @@
             vmem_limit_bytes=16 * 2**20, collective_id=0, has_side_effects=True
         ),
         name="section",
-    )(solid_state, material, ocean_state, ocean_medium, offset_x.reshape(1, -1), offset_y.reshape(1, -1))
+    )(*(
+        pltpu.with_memory_space_constraint(a, pltpu.HBM)
+        for a in (solid_state, material, ocean_state, ocean_medium, offset_x.reshape(1, -1), offset_y.reshape(1, -1))
+    ))
     return pl.pallas_call(
         write_kernel,
         out_shape=[jax.ShapeDtypeStruct(shape, F32) for shape in outs],

time: 24.6 us -> 17.9 us (0.73)
  the two profiles are of different devices: /device:TPU:1 before, /device:TPU:39 now
where the time goes in v2:
time: 17.9 us; the launch traced here: 17.8 us
  Pallas kernels  17.2 us (96%)
  between operations  0.64 us (4%)
    pallas_call x1, Pallas kernels, body(): pl.pallas_call(functools.partial(section_kernel, sizes), out_shape=[pltpu...  16 us
    pallas_call x1, Pallas kernels, body(): pl.pallas_call(write_kernel, out_shape=[jax.ShapeDtypeStruct(shape, F32)...  1.2 us

profile of v2, /device:TPU:39, one launch (start us, length us, event | category | flops | bytes accessed | tf_op | source)
XLA Modules:
  0.0 17.8 jit_solution(4522427014499673336)
XLA Ops:
  0.6 16.0 %section.1 = (f32[9,8,8,128]{3,2,1,0:T(8,128)S(1)}, f32[9,8,8,128]{3,2,1,0:T(8,128)S(1)}, f32[4,16,16,64]{3,2,1,0:T(8,128)S(1)}, f32[4,16,16,64]{3,2,1,0:T(8,128)S(1)}) custom-call(f32[9,8,8,128]{3,2,1,0:T(8,128)} %solid.1, f32[4,8,8,128]{3,2,1,0:T(8,128)} %material.1, f32[4,16,16,64]{3,2,1,0:T(8,128)} %ocean.1, f32[2,16]{1,0:T(2,128)} %medium.1, ...), custom_call_target="tpu_custom_call" | custom-call | tf_op jit(solution)/shard_map/section/pallas_call | solution.py:502
  16.6 1.2 %write_out.1 = (f32[9,8,8,128]{3,2,1,0:T(8,128)}, f32[9,8,8,128]{3,2,1,0:T(8,128)}, f32[4,16,16,64]{3,2,1,0:T(8,128)}, f32[4,16,16,64]{3,2,1,0:T(8,128)}) custom-call(f32[9,8,8,128]{3,2,1,0:T(8,128)S(1)} %get-tuple-element.8.refs_0_, f32[9,8,8,128]{3,2,1,0:T(8,128)S(1)} %get-tuple-element.9.refs_1_, f32[4,16,16,64]{3,2,1,0:T(8,128)S(1)} %get-tuple-element.10.refs_2_, ...), custom_call_target="tpu_custom_call" | custom-call | tf_op jit(solution)/shard_map/write_out/pallas_call | solution.py:523

commit v3 on v2

--- a/solution.py
+++ b/solution.py
@@ -115,15 +115,19 @@
     when(pred, lambda: [copy.wait_send() for copy in copies] and None)
 
 
+def both(a, b):
+    return jnp.logical_and(a, b)
+
+
 def section_kernel(
     sizes,
     solid, material, ocean, medium, off_x, off_y,
     s_next, s_rate, o_next, o_rate,
     sb, mb, ob, ov, med, ox, oy,
     z_low, z_high, plane, bed_part,
-    ys_out, ys_left, ys_right, yo_out, yo_left, yo_right, coarse_out,
+    xo_out, xo_low, xo_high, ys_out, ys_left, ys_right, yo_out, yo_left, yo_right, coarse_out,
     dys, dyo, dzs, txs, opre, cat,
-    local_sem, send_sem, recv_sem,
+    local_sem, send_sem, recv_sem, there,
 ):
     nx, ny, nz = sizes
     gx, gy, gz = lax.axis_index("gx"), lax.axis_index("gy"), lax.axis_index("gz")
@@ -136,31 +140,37 @@
     left = (gx, jnp.where(z_first, down_y, gy), jnp.where(z_first, nz - 1, gz - 1))
     xs = {-1: down_x, 0: gx, 1: up_x}
 
-    barrier = pltpu.get_barrier_semaphore()
-
-    def greet(x, y, z):
-        pl.semaphore_signal(barrier, inc=1, device_id=(x, y, z), device_id_type=MESH)
-
     x_down, x_up = gx > 0, gx < nx - 1
     y_down, y_up = gy > 0, gy < ny - 1
     z_down, z_up = gz > 0, gz < nz - 1
     has_left, has_right = jnp.logical_or(y_down, z_down), jnp.logical_or(y_up, z_up)
-    both = jnp.logical_and
     has = {-1: x_down, 1: x_up}
 
-    when(x_up, lambda: greet(up_x, gy, gz))
-    when(x_down, lambda: greet(down_x, gy, gz))
+    run = max(nx // 4, 2)
+    turn = lax.rem(gx, run)
+    late = {1: turn < run // 2, -1: jnp.logical_or(turn == 0, turn > run // 2)}
+    has_late = {e: both(has[e], late[e]) for e in (-1, 1)}
+    has_early = {e: both(has[e], jnp.logical_not(late[e])) for e in (-1, 1)}
+    odd = lax.rem(gz, 2) == 1
+    even = jnp.logical_not(odd)
+    barrier = pltpu.get_barrier_semaphore()
+
+    def greet(x, y, z):
+        pl.semaphore_signal(barrier, inc=1, device_id=(x, y, z), device_id_type=MESH)
+
+    def tell(index, x, y, z):
+        pl.semaphore_signal(there.at[index], inc=1, device_id=(x, y, z), device_id_type=MESH)
+
+    plane[...] = jnp.zeros_like(plane)
+    for e in (-1, 1):
+        when(has_late[e], lambda: greet(xs[e], gy, gz))
     when(y_up, lambda: greet(gx, up_y, gz))
-    when(y_down, lambda: greet(gx, down_y, gz))
-    when(has_right, lambda: greet(*right))
-    when(has_left, lambda: greet(*left))
-    for k in range(2, nz):
-        when(z_first, lambda: greet(gx, gy, k))
-    when(gz > 1, lambda: greet(gx, gy, 0))
+    when(odd, lambda: greet(gx, gy, gz - 1))
+    when(gz < 2, lambda: greet(gx, gy, 2))
     for e in (-1, 1):
-        when(both(has[e], z_down), lambda: greet(xs[e], gy, 0))
-        when(both(has[e], both(z_first, y_down)), lambda: greet(xs[e], down_y, 0))
-        when(both(has[e], both(z_last, y_up)), lambda: greet(xs[e], up_y, 0))
+        when(both(has_late[e], z_down), lambda: greet(xs[e], gy, 0))
+        when(both(has_late[e], both(z_first, y_down)), lambda: greet(xs[e], down_y, 0))
+        when(both(has_late[e], both(z_last, y_up)), lambda: greet(xs[e], up_y, 0))
 
     loads = [
         pltpu.make_async_copy(src, dst, local_sem.at[i])
@@ -185,20 +195,29 @@
 
     when(z_first, lambda: clear(z_low))
     when(z_last, lambda: clear(z_high))
-    when(x_first, lambda: clear(sb.at[:, :, 6:8], ob.at[:, :, 6:8], plane.at[:, 0]))
-    when(x_last, lambda: clear(sb.at[:, :, 16:18], ob.at[:, :, 24:26], plane.at[:, 2]))
+    when(x_first, lambda: clear(sb.at[:, :, 6:8], xo_low))
+    when(x_last, lambda: clear(sb.at[:, :, 16:18], xo_high))
     when(y_first, lambda: clear(ys_left))
     when(y_last, lambda: clear(ys_right))
-    when(jnp.logical_not(has_left), lambda: clear(yo_left, plane.at[1]))
-    when(jnp.logical_not(has_right), lambda: clear(yo_right, plane.at[1]))
+    when(jnp.logical_not(has_left), lambda: clear(yo_left))
+    when(jnp.logical_not(has_right), lambda: clear(yo_right))
 
     def count(*preds):
         return sum(jnp.where(p, 1, 0) for p in preds)
 
-    n_x, n_y = count(x_down, x_up), count(y_down, y_up)
-    n_side = count(has_left, has_right)
-    first_extra = (nz - 2) + n_x * (nz - 1 + n_y)
-    pl.semaphore_wait(barrier, n_x + n_y + n_side + jnp.where(z_first, first_extra, jnp.where(gz > 1, 1, 0)))
+    n_early = count(*has_early.values())
+    n_y = count(y_down, y_up)
+    n_greet = count(y_down, even) + jnp.where(gz == 2, 2, 0)
+    n_greet = n_greet + n_early * (1 + jnp.where(z_first, nz - 1 + n_y, 0))
+    when(n_greet > 0, lambda: pl.semaphore_wait(barrier, n_greet))
+    for e, index in ((1, 1), (-1, 0)):
+        when(has_early[e], lambda: tell(index, xs[e], gy, gz))
+    when(y_down, lambda: tell(2, gx, down_y, gz))
+    when(gz == 2, lambda: tell(3, gx, gy, 1))
+    when(even, lambda: tell(4, gx, gy, gz + 1))
+    when(gz == 2, lambda: tell(5, gx, gy, 0))
+    def await_partner(pred, index, amount=1):
+        when(pred, lambda: pl.semaphore_wait(there.at[index], amount))
 
     counter = iter(range(64))
 
@@ -212,10 +231,10 @@
     for i, (a, b) in enumerate(((0, 4), (7, 9))):
         up_copies.append(remote(solid.at[a:b, :, 6:8], sb.at[a:b, :, 6:8], 2 * i, (up_x, gy, gz)))
         down_copies.append(remote(solid.at[a:b, :, 0:2], sb.at[a:b, :, 16:18], 2 * i + 1, (down_x, gy, gz)))
-    up_copies.append(remote(ocean.at[0:2, :, 14:16], ob.at[:, :, 6:8], 4, (up_x, gy, gz)))
-    down_copies.append(remote(ocean.at[0:2, :, 0:2], ob.at[:, :, 24:26], 5, (down_x, gy, gz)))
-    start(x_up, *up_copies)
-    start(x_down, *down_copies)
+    wave_up = remote(xo_out.at[1], xo_low, 4, (up_x, gy, gz))
+    wave_down = remote(xo_out.at[0], xo_high, 5, (down_x, gy, gz))
+    start(has_early[1], *up_copies)
+    start(has_early[-1], *down_copies)
 
     z_up_copies = [
         remote(solid.at[a : a + 3, 6:8], z_low.at[b : b + 3], 6 + i, (gx, gy, gz + 1))
@@ -225,24 +244,37 @@
         remote(solid.at[a : a + 3, 0:2], z_high.at[b : b + 3], 8 + i, (gx, gy, gz - 1))
         for i, (a, b) in enumerate(((0, 0), (5, 3)))
     ]
-    start(z_up, *z_up_copies)
-    start(z_down, *z_down_copies)
 
     tile = solid.at[2, 0]
-    plane_copies = []
+    plane_early, plane_late = [], []
+    rows = {-1: slice(7, 8), 0: slice(0, 8), 1: slice(0, 1)}
     for e in (-1, 0, 1):
-        x = xs[-e]
-        there = z_first if e == 0 else both(z_first, has[-e])
-        mine = [remote(tile, plane.at[0, e + 1], 10 + e + 1, (x, gy, k)) for k in range(1 if e == 0 else 0, nz)]
-        plane_copies.append((there, mine))
-        plane_copies.append((both(there, y_up), [remote(tile, plane.at[1, e + 1], 13 + e + 1, (x, up_y, 0))]))
-        plane_copies.append((both(there, y_down), [remote(tile, plane.at[1, e + 1], 13 + e + 1, (x, down_y, nz - 1))]))
+        x, r = xs[-e], rows[e]
+        part = solid.at[2, 0, r]
+        mine = [remote(part, plane.at[0, e + 1, r], 10 + e + 1, (x, gy, k)) for k in range(1 if e == 0 else 0, nz)]
+        above = remote(part, plane.at[1, e + 1, r], 13 + e + 1, (x, up_y, 0))
+        below = remote(part, plane.at[1, e + 1, r], 13 + e + 1, (x, down_y, nz - 1))
+        if e == 0:
+            plane_early += [(z_first, mine[:1])]
+            plane_late += [(z_first, mine[1:]), (both(z_first, y_up), [above]), (both(z_first, y_down), [below])]
+        else:
+            pred = both(z_first, has_early[-e])
+            plane_early += [(pred, mine), (both(pred, y_up), [above]), (both(pred, y_down), [below])]
+    plane_on = {
+        e: remote(plane.at[0, 1, rows[-e]], plane.at[0, 1 - e, rows[-e]], 11 - e, (xs[e], gy, gz)) for e in (-1, 1)
+    }
     own_plane = pltpu.make_async_copy(tile, plane.at[0, 1], local_sem.at[7])
     when(z_first, own_plane.start)
-    for pred, copies in plane_copies:
+    for pred, copies in plane_early:
         start(pred, *copies)
 
     lane = lax.broadcasted_iota(jnp.int32, (8, 128), 1)
+
+    loads[1].wait()
+    for end, row in ((0, 8), (1, 22)):
+        xo_out[end] = jnp.concatenate([ob[0, :, row : row + 2, :], ob[1, :, row : row + 2, :]], axis=2)
+    start(has_early[1], wave_up)
+    start(has_early[-1], wave_down)
 
     loads[0].wait()
     for half, fields in enumerate((y_fields[:4], y_fields[4:])):
@@ -256,10 +288,8 @@
         remote(ys_out, ys_left, 16, (gx, up_y, gz)),
         remote(ys_out, ys_right, 17, (gx, down_y, gz)),
     ]
-    start(y_up, ys_copies[0])
     start(y_down, ys_copies[1])
 
-    loads[1].wait()
     loads[2].wait()
     half_lane = lax.rem(lane, 64)
     for i in range(2):
@@ -273,8 +303,8 @@
             packed = jnp.where(half_lane // 4 == d, roll_lanes(folded, 4 * d + 2), packed)
         yo_out[i] = packed
     yo_copies = [remote(yo_out, yo_left, 18, right), remote(yo_out, yo_right, 19, left)]
-    start(has_right, yo_copies[0])
-    start(has_left, yo_copies[1])
+    start(both(even, has_right), yo_copies[0])
+    start(gz == 2, yo_copies[1])
 
     row = lax.broadcasted_iota(jnp.int32, (8, 16), 0)
     col = lax.broadcasted_iota(jnp.int32, (8, 16), 1)
@@ -286,8 +316,7 @@
     coarse = jnp.dot(coarse, place, precision=HIGHEST, preferred_element_type=F32)
     coarse_out[...] = coarse
     coarse_copies = [remote(coarse_out, bed_part.at[k], 20 + k, (gx, gy, 0)) for k in range(1, nz)]
-    for k in range(1, nz):
-        start(gz == k, coarse_copies[k - 1])
+    start(gz == 2, coarse_copies[1])
 
     wy = weights(lane, 128, y_first, y_last, True)
     for i, f in enumerate(y_fields):
@@ -303,6 +332,50 @@
     for i, f in enumerate(x_fields):
         own = sb[f, :, 8:16, :]
         txs[i] = wx[0] * own + wx[3] * pltpu.roll(own, 5, 1) + wx[-3] * pltpu.roll(own, 3, 1)
+
+    start(even, *z_up_copies)
+    start(gz == 2, *z_down_copies)
+    await_partner(odd, 4)
+    start(odd, *z_down_copies, yo_copies[1])
+    for k in (1, 3):
+        start(gz == k, coarse_copies[k - 1])
+    await_partner(gz == 1, 3)
+    start(gz == 1, *z_up_copies, yo_copies[0])
+    await_partner(z_first, 5)
+    start(*plane_late[0][:1], *plane_late[0][1])
+    await_partner(y_up, 2)
+    start(y_up, ys_copies[0])
+    when(both(z_first, y_up), lambda: tell(7, gx, gy, nz - 1))
+    when(both(z_first, y_up), lambda: tell(6, gx, up_y, 0))
+    start(*plane_late[1][:1], *plane_late[1][1])
+    await_partner(both(z_first, y_down), 6)
+    start(both(z_first, y_down), yo_copies[1], *plane_late[2][1])
+    await_partner(both(z_last, y_up), 7)
+    start(both(z_last, y_up), yo_copies[0])
+    for e, index, copies in ((1, 0, up_copies + [wave_up]), (-1, 1, down_copies + [wave_down])):
+        await_partner(has_late[e], index)
+        start(has_late[e], *copies)
+    sides = ((both(z_first, y_down), 127), (both(z_last, y_up), 0))
+
+    def plane_wait(s, e):
+        pltpu.make_async_remote_copy(
+            src_ref=solid.at[2, 0, rows[e]], dst_ref=plane.at[s, e + 1, rows[e]], send_sem=send_sem.at[63], recv_sem=recv_sem.at[10 + 3 * s + e + 1],
+            device_id=(gx, up_y, gz), device_id_type=MESH,
+        ).wait_recv()
+
+    def merge(e):
+        for pred, at in sides:
+
+            @pl.when(pred)
+            def _(at=at):
+                plane_wait(1, e)
+                plane[0, e + 1] = jnp.where(lane == at, plane[1, e + 1], plane[0, e + 1])
+
+    when(z_first, own_plane.wait)
+    when(z_down, lambda: plane_wait(0, 0))
+    merge(0)
+    for e in (-1, 1):
+        start(has_late[e], plane_on[e])
 
     landed(y_down, ys_copies[0])
     landed(y_up, ys_copies[1])
@@ -354,46 +427,6 @@
         dzs[4, 0] += scale * sb[6, 0, 8:16, :]
         dzs[3, 0] += scale * (sb[5, 0, 8:16, :] + bed_pressure)
 
-    loads[5].wait()
-    loads[6].wait()
-
-    def plane_wait(s, e):
-        pltpu.make_async_remote_copy(
-            src_ref=tile, dst_ref=plane.at[s, e + 1], send_sem=send_sem.at[63], recv_sem=recv_sem.at[10 + 3 * s + e + 1],
-            device_id=(gx, up_y, gz), device_id_type=MESH,
-        ).wait_recv()
-
-    when(z_first, own_plane.wait)
-    when(z_down, lambda: plane_wait(0, 0))
-    for e in (-1, 1):
-        when(has[e], lambda: plane_wait(0, e))
-    for pred, at in ((both(z_first, y_down), 127), (both(z_last, y_up), 0)):
-        when(pred, lambda: plane_wait(1, 0))
-        for e in (-1, 1):
-            when(both(pred, has[e]), lambda: plane_wait(1, e))
-
-        @pl.when(pred)
-        def _(at=at):
-            for e in range(3):
-                plane[0, e] = jnp.where(lane == at, plane[1, e], plane[0, e])
-
-    window = plane[0].reshape(24, 128)
-    fine_x = lax.broadcasted_iota(jnp.int32, (24, 16), 1)
-    coarse_x = lax.broadcasted_iota(jnp.int32, (24, 16), 0) + (8 * gx - 8)
-    near_x = 8 * gx + fine_x // 2
-    far_x = jnp.clip(near_x + ox[...], 0, 8 * nx - 1)
-    blend_x = jnp.where(coarse_x == near_x, 0.75, 0.0) + jnp.where(coarse_x == far_x, 0.25, 0.0)
-    fine_y = lax.broadcasted_iota(jnp.int32, (128, 64), 1)
-    coarse_y = lax.broadcasted_iota(jnp.int32, (128, 64), 0)
-    near_y = 128 * gy + 32 * gz + fine_y // 2
-    far_y = jnp.clip(near_y + oy[...], 0, 128 * ny - 1)
-    blend_y = jnp.where(coarse_y == lax.rem(near_y, 128), 0.75, 0.0)
-    blend_y = blend_y + jnp.where(coarse_y == lax.rem(far_y, 128), 0.25, 0.0)
-    bed_speed = lax.dot_general(
-        blend_x, window, (((0,), (0,)), ((), ())), precision=HIGHEST, preferred_element_type=F32
-    )
-    bed_speed = jnp.dot(bed_speed, blend_y, precision=HIGHEST, preferred_element_type=F32)
-
     loads[4].wait()
 
     def unfold(i, d):
@@ -408,8 +441,6 @@
         dz_w = total(w * ov[1, d + k] for k, w in table.items())
         dz_p = total(w * ob[0, d + k, 8:24, :] for k, w in table.items())
         part = -bulk * (2.0 * unfold(1, d) + dz_w) + gravity * flow_w / light
-        if d == 15:
-            part = part + inv_norm * bulk * (flow_w - bed_speed)
         opre[d] = step_size * part
         rate_v = (-2.0 * step_size) * light * unfold(0, d)
         rate_w = -light * dz_p
@@ -421,8 +452,11 @@
         o_next[2, d] = flow_v + section_weight * rate_v
         o_next[3, d] = flow_w + section_weight * rate_w
 
-    landed(x_down, *up_copies)
-    landed(x_up, *down_copies)
+    landed(x_down, *up_copies, wave_up)
+    landed(x_up, *down_copies, wave_down)
+    for rim, row in ((xo_low, 6), (xo_high, 24)):
+        for i in range(2):
+            ob[i, :, row : row + 2, :] = rim[:, :, 64 * i : 64 * i + 64]
 
     def dx(i, f, z):
         out = txs[i, z]
@@ -462,25 +496,57 @@
         out = out + wp[3] * jnp.where(far_up, ob[i, d, 11:27, :], 0.0)
         return out + wp[-3] * jnp.where(far_down, ob[i, d, 5:21, :], 0.0)
 
+    def ocean_out(i, d, rate):
+        o_rate[i, d] = rate
+        o_next[i, d] = ob[i, d, 8:24, :] + section_weight * rate
+
     for d in range(16):
         bulk = jnp.full((16, 64), (-2.0 * step_size) * med[0, d], F32)
         light = jnp.full((16, 64), (-2.0 * step_size) * med[1, d], F32)
         rate_p = opre[d] + bulk * dx_ocean(1, d)
-        rate_u = light * dx_ocean(0, d)
-        o_rate[0, d] = rate_p
-        o_rate[1, d] = rate_u
-        o_next[0, d] = ob[0, d, 8:24, :] + section_weight * rate_p
-        o_next[1, d] = ob[1, d, 8:24, :] + section_weight * rate_u
-
-    sent(x_up, *up_copies)
-    sent(x_down, *down_copies)
+        ocean_out(1, d, light * dx_ocean(0, d))
+        if d < 15:
+            ocean_out(0, d, rate_p)
+
+    loads[5].wait()
+    loads[6].wait()
+    for e in (-1, 1):
+        when(has[e], lambda: plane_wait(0, e))
+        when(has_late[e], lambda: merge(e))
+
+    window = plane[0].reshape(24, 128)
+    fine_x = lax.broadcasted_iota(jnp.int32, (24, 16), 1)
+    coarse_x = lax.broadcasted_iota(jnp.int32, (24, 16), 0) + (8 * gx - 8)
+    near_x = 8 * gx + fine_x // 2
+    far_x = jnp.clip(near_x + ox[...], 0, 8 * nx - 1)
+    blend_x = jnp.where(coarse_x == near_x, 0.75, 0.0) + jnp.where(coarse_x == far_x, 0.25, 0.0)
+    fine_y = lax.broadcasted_iota(jnp.int32, (128, 64), 1)
+    coarse_y = lax.broadcasted_iota(jnp.int32, (128, 64), 0)
+    near_y = 128 * gy + 32 * gz + fine_y // 2
+    far_y = jnp.clip(near_y + oy[...], 0, 128 * ny - 1)
+    blend_y = jnp.where(coarse_y == lax.rem(near_y, 128), 0.75, 0.0)
+    blend_y = blend_y + jnp.where(coarse_y == lax.rem(far_y, 128), 0.25, 0.0)
+    bed_speed = lax.dot_general(
+        blend_x, window, (((0,), (0,)), ((), ())), precision=HIGHEST, preferred_element_type=F32
+    )
+    bed_speed = jnp.dot(bed_speed, blend_y, precision=HIGHEST, preferred_element_type=F32)
+
+    bulk = jnp.full((16, 64), (step_size * inv_norm) * med[0, 15], F32)
+    ocean_out(0, 15, rate_p + bulk * (ov[1, 15] - bed_speed))
+
+    sent(x_up, *up_copies, wave_up)
+    sent(x_down, *down_copies, wave_down)
+    for e in (-1, 1):
+        sent(has_late[e], plane_on[e])
     sent(y_up, ys_copies[0])
     sent(y_down, ys_copies[1])
     sent(has_right, yo_copies[0])
     sent(has_left, yo_copies[1])
     sent(z_up, *z_up_copies)
     sent(z_down, *z_down_copies)
-    for pred, copies in plane_copies:
+    for pred, copies in plane_late:
+        sent(pred, *copies)
+    for pred, copies in plane_early:
         sent(pred, *copies)
     for k in range(1, nz):
         sent(gz == k, coarse_copies[k - 1])
@@ -508,9 +574,11 @@
             v(9, 8, 24, 128), v(4, 8, 8, 128), v(2, 16, 32, 64), v(2, 16, 16, 64),
             pltpu.SMEM((2, 16), F32), pltpu.VMEM((1, 16), jnp.int32), pltpu.VMEM((1, 64), jnp.int32),
             v(6, 2, 8, 128), v(6, 2, 8, 128), v(2, 3, 8, 128), v(4, 8, 128),
+            v(2, 16, 2, 128), v(16, 2, 128), v(16, 2, 128),
             v(2, 8, 128), v(2, 8, 128), v(2, 8, 128), v(2, 8, 128), v(2, 8, 128), v(2, 8, 128), v(8, 128),
             v(6, 8, 8, 128), v(2, 16, 8, 128), v(6, 8, 8, 128), v(6, 8, 8, 128), v(16, 16, 64), v(2, 16, 8, 128),
             pltpu.SemaphoreType.DMA((8,)), pltpu.SemaphoreType.DMA((64,)), pltpu.SemaphoreType.DMA((24,)),
+            pltpu.SemaphoreType.REGULAR((8,)),
         ],
         compiler_params=pltpu.CompilerParams(
             vmem_limit_bytes=16 * 2**20, collective_id=0, has_side_effects=True

time: 17.9 us -> 15.6 us (0.87)
  the two profiles are of different devices: /device:TPU:39 before, /device:TPU:30 now
where the time goes in v3:
time: 15.6 us; the launch traced here: 15.5 us
  Pallas kernels  14.8 us (95%)
  between operations  0.64 us (4%)
    pallas_call x1, Pallas kernels, body(): pl.pallas_call(functools.partial(section_kernel, sizes), out_shape=[pltpu...  13.6 us
    pallas_call x1, Pallas kernels, body(): pl.pallas_call(write_kernel, out_shape=[jax.ShapeDtypeStruct(shape, F32)...  1.2 us

profile of v3, /device:TPU:30, one launch (start us, length us, event | category | flops | bytes accessed | tf_op | source)
XLA Modules:
  0.0 15.5 jit_solution(849483902538776376)
XLA Ops:
  0.6 13.6 %section.1 = (f32[9,8,8,128]{3,2,1,0:T(8,128)S(1)}, f32[9,8,8,128]{3,2,1,0:T(8,128)S(1)}, f32[4,16,16,64]{3,2,1,0:T(8,128)S(1)}, f32[4,16,16,64]{3,2,1,0:T(8,128)S(1)}) custom-call(f32[9,8,8,128]{3,2,1,0:T(8,128)} %solid.1, f32[4,8,8,128]{3,2,1,0:T(8,128)} %material.1, f32[4,16,16,64]{3,2,1,0:T(8,128)} %ocean.1, f32[2,16]{1,0:T(2,128)} %medium.1, ...), custom_call_target="tpu_custom_call" | custom-call | tf_op jit(solution)/shard_map/section/pallas_call | solution.py:568
  14.3 1.2 %write_out.1 = (f32[9,8,8,128]{3,2,1,0:T(8,128)}, f32[9,8,8,128]{3,2,1,0:T(8,128)}, f32[4,16,16,64]{3,2,1,0:T(8,128)}, f32[4,16,16,64]{3,2,1,0:T(8,128)}) custom-call(f32[9,8,8,128]{3,2,1,0:T(8,128)S(1)} %get-tuple-element.8.refs_0_, f32[9,8,8,128]{3,2,1,0:T(8,128)S(1)} %get-tuple-element.9.refs_1_, f32[4,16,16,64]{3,2,1,0:T(8,128)S(1)} %get-tuple-element.10.refs_2_, ...), custom_call_target="tpu_custom_call" | custom-call | tf_op jit(solution)/shard_map/write_out/pallas_call | solution.py:591

commit v4 on v3

--- a/solution.py
+++ b/solution.py
@@ -151,6 +151,9 @@
     late = {1: turn < run // 2, -1: jnp.logical_or(turn == 0, turn > run // 2)}
     has_late = {e: both(has[e], late[e]) for e in (-1, 1)}
     has_early = {e: both(has[e], jnp.logical_not(late[e])) for e in (-1, 1)}
+    far_up, far_down = both(y_up, gy == ny - 2), both(y_down, gy == ny - 1)
+    y_up_word, y_down_word = both(far_up, gz < 2), both(far_down, gz < 2)
+    y_up_near, y_down_near = both(y_up, jnp.logical_not(y_up_word)), both(y_down, jnp.logical_not(y_down_word))
     odd = lax.rem(gz, 2) == 1
     even = jnp.logical_not(odd)
     barrier = pltpu.get_barrier_semaphore()
@@ -162,9 +165,9 @@
         pl.semaphore_signal(there.at[index], inc=1, device_id=(x, y, z), device_id_type=MESH)
 
     plane[...] = jnp.zeros_like(plane)
+    when(y_up_near, lambda: greet(gx, up_y, gz))
     for e in (-1, 1):
         when(has_late[e], lambda: greet(xs[e], gy, gz))
-    when(y_up, lambda: greet(gx, up_y, gz))
     when(odd, lambda: greet(gx, gy, gz - 1))
     when(gz < 2, lambda: greet(gx, gy, 2))
     for e in (-1, 1):
@@ -207,12 +210,12 @@
 
     n_early = count(*has_early.values())
     n_y = count(y_down, y_up)
-    n_greet = count(y_down, even) + jnp.where(gz == 2, 2, 0)
+    n_greet = count(y_down_near, even) + jnp.where(gz == 2, 2, 0)
     n_greet = n_greet + n_early * (1 + jnp.where(z_first, nz - 1 + n_y, 0))
     when(n_greet > 0, lambda: pl.semaphore_wait(barrier, n_greet))
     for e, index in ((1, 1), (-1, 0)):
         when(has_early[e], lambda: tell(index, xs[e], gy, gz))
-    when(y_down, lambda: tell(2, gx, down_y, gz))
+    when(y_down_near, lambda: tell(2, gx, down_y, gz))
     when(gz == 2, lambda: tell(3, gx, gy, 1))
     when(even, lambda: tell(4, gx, gy, gz + 1))
     when(gz == 2, lambda: tell(5, gx, gy, 0))
@@ -288,7 +291,7 @@
         remote(ys_out, ys_left, 16, (gx, up_y, gz)),
         remote(ys_out, ys_right, 17, (gx, down_y, gz)),
     ]
-    start(y_down, ys_copies[1])
+    start(y_down_near, ys_copies[1])
 
     loads[2].wait()
     half_lane = lax.rem(lane, 64)
@@ -343,12 +346,19 @@
     start(gz == 1, *z_up_copies, yo_copies[0])
     await_partner(z_first, 5)
     start(*plane_late[0][:1], *plane_late[0][1])
-    await_partner(y_up, 2)
+    await_partner(y_up_near, 2)
+    near_link = both(z_first, y_up_near)
+    far_link = both(far_up, gz == 2)
+    when(jnp.logical_or(near_link, far_link), lambda: tell(7, gx, gy, nz - 1))
+    when(jnp.logical_or(near_link, far_link), lambda: tell(6, gx, up_y, 0))
+    when(far_link, lambda: tell(6, gx, up_y, 1))
+    for k in (0, 1):
+        when(far_link, lambda: tell(7, gx, gy, k))
+    await_partner(y_up_word, 7)
     start(y_up, ys_copies[0])
-    when(both(z_first, y_up), lambda: tell(7, gx, gy, nz - 1))
-    when(both(z_first, y_up), lambda: tell(6, gx, up_y, 0))
     start(*plane_late[1][:1], *plane_late[1][1])
-    await_partner(both(z_first, y_down), 6)
+    await_partner(jnp.logical_or(both(z_first, y_down), y_down_word), 6)
+    start(y_down_word, ys_copies[1])
     start(both(z_first, y_down), yo_copies[1], *plane_late[2][1])
     await_partner(both(z_last, y_up), 7)
     start(both(z_last, y_up), yo_copies[0])

time: 15.6 us -> 14.1 us (0.904)
  the two profiles are of different devices: /device:TPU:30 before, /device:TPU:14 now
where the time goes in v4:
time: 14.1 us; the launch traced here: 14 us
  Pallas kernels  13.4 us (95%)
  between operations  0.64 us (5%)
    pallas_call x1, Pallas kernels, body(): pl.pallas_call(functools.partial(section_kernel, sizes), out_shape=[pltpu...  12.2 us
    pallas_call x1, Pallas kernels, body(): pl.pallas_call(write_kernel, out_shape=[jax.ShapeDtypeStruct(shape, F32)...  1.2 us

profile of v4, /device:TPU:14, one launch (start us, length us, event | category | flops | bytes accessed | tf_op | source)
XLA Modules:
  0.0 14.0 jit_solution(9963250460659063287)
XLA Ops:
  0.6 12.2 %section.1 = (f32[9,8,8,128]{3,2,1,0:T(8,128)S(1)}, f32[9,8,8,128]{3,2,1,0:T(8,128)S(1)}, f32[4,16,16,64]{3,2,1,0:T(8,128)S(1)}, f32[4,16,16,64]{3,2,1,0:T(8,128)S(1)}) custom-call(f32[9,8,8,128]{3,2,1,0:T(8,128)} %solid.1, f32[4,8,8,128]{3,2,1,0:T(8,128)} %material.1, f32[4,16,16,64]{3,2,1,0:T(8,128)} %ocean.1, f32[2,16]{1,0:T(2,128)} %medium.1, ...), custom_call_target="tpu_custom_call" | custom-call | tf_op jit(solution)/shard_map/section/pallas_call | solution.py:578
  12.8 1.2 %write_out.1 = (f32[9,8,8,128]{3,2,1,0:T(8,128)}, f32[9,8,8,128]{3,2,1,0:T(8,128)}, f32[4,16,16,64]{3,2,1,0:T(8,128)}, f32[4,16,16,64]{3,2,1,0:T(8,128)}) custom-call(f32[9,8,8,128]{3,2,1,0:T(8,128)S(1)} %get-tuple-element.8.refs_0_, f32[9,8,8,128]{3,2,1,0:T(8,128)S(1)} %get-tuple-element.9.refs_1_, f32[4,16,16,64]{3,2,1,0:T(8,128)S(1)} %get-tuple-element.10.refs_2_, ...), custom_call_target="tpu_custom_call" | custom-call | tf_op jit(solution)/shard_map/write_out/pallas_call | solution.py:601

commit v5 on v4

--- a/solution.py
+++ b/solution.py
@@ -122,11 +122,11 @@
 def section_kernel(
     sizes,
     solid, material, ocean, medium, off_x, off_y,
-    s_next, s_rate, o_next, o_rate,
-    sb, mb, ob, ov, med, ox, oy,
+    o_next, o_rate, sb, mb, txs, dys, dzs,
+    ob, ov, med, ox, oy,
     z_low, z_high, plane, bed_part,
     xo_out, xo_low, xo_high, ys_out, ys_left, ys_right, yo_out, yo_left, yo_right, coarse_out,
-    dys, dyo, dzs, txs, opre, cat,
+    dyo, opre, cat,
     local_sem, send_sem, recv_sem, there,
 ):
     nx, ny, nz = sizes
@@ -189,8 +189,8 @@
             )
         )
     ]
-    for load in loads:
-        load.start()
+    for i in (1, 0, 2, 3, 4, 5, 6):
+        loads[i].start()
 
     def clear(*places):
         for ref in places:
@@ -236,8 +236,8 @@
         down_copies.append(remote(solid.at[a:b, :, 0:2], sb.at[a:b, :, 16:18], 2 * i + 1, (down_x, gy, gz)))
     wave_up = remote(xo_out.at[1], xo_low, 4, (up_x, gy, gz))
     wave_down = remote(xo_out.at[0], xo_high, 5, (down_x, gy, gz))
-    start(has_early[1], *up_copies)
-    start(has_early[-1], *down_copies)
+    start(has_early[1], up_copies[0])
+    start(has_early[-1], down_copies[0])
 
     z_up_copies = [
         remote(solid.at[a : a + 3, 6:8], z_low.at[b : b + 3], 6 + i, (gx, gy, gz + 1))
@@ -270,6 +270,9 @@
     when(z_first, own_plane.start)
     for pred, copies in plane_early:
         start(pred, *copies)
+
+    start(has_early[1], up_copies[1])
+    start(has_early[-1], down_copies[1])
 
     lane = lax.broadcasted_iota(jnp.int32, (8, 128), 1)
 
@@ -462,11 +465,88 @@
         o_next[2, d] = flow_v + section_weight * rate_v
         o_next[3, d] = flow_w + section_weight * rate_w
 
+    loads[5].wait()
+    loads[6].wait()
+    fine_x = lax.broadcasted_iota(jnp.int32, (24, 16), 1)
+    coarse_x = lax.broadcasted_iota(jnp.int32, (24, 16), 0) + (8 * gx - 8)
+    near_x = 8 * gx + fine_x // 2
+    far_x = jnp.clip(near_x + ox[...], 0, 8 * nx - 1)
+    blend_x = jnp.where(coarse_x == near_x, 0.75, 0.0) + jnp.where(coarse_x == far_x, 0.25, 0.0)
+    fine_y = lax.broadcasted_iota(jnp.int32, (128, 64), 1)
+    coarse_y = lax.broadcasted_iota(jnp.int32, (128, 64), 0)
+    near_y = 128 * gy + 32 * gz + fine_y // 2
+    far_y = jnp.clip(near_y + oy[...], 0, 128 * ny - 1)
+    blend_y = jnp.where(coarse_y == lax.rem(near_y, 128), 0.75, 0.0)
+    blend_y = blend_y + jnp.where(coarse_y == lax.rem(far_y, 128), 0.25, 0.0)
+
     landed(x_down, *up_copies, wave_up)
     landed(x_up, *down_copies, wave_down)
     for rim, row in ((xo_low, 6), (xo_high, 24)):
         for i in range(2):
             ob[i, :, row : row + 2, :] = rim[:, :, 64 * i : 64 * i + 64]
+
+    pos = lax.broadcasted_iota(jnp.int32, (16, 64), 0)
+    wp = weights(pos, 16, x_first, x_last, False)
+    far_up, far_down = wp[3] != 0.0, wp[-3] != 0.0
+
+    def dx_ocean(i, d):
+        out = total(wp[k] * ob[i, d, 8 + k : 24 + k, :] for k in range(-2, 3))
+        out = out + wp[3] * jnp.where(far_up, ob[i, d, 11:27, :], 0.0)
+        return out + wp[-3] * jnp.where(far_down, ob[i, d, 5:21, :], 0.0)
+
+    def ocean_out(i, d, rate):
+        o_rate[i, d] = rate
+        o_next[i, d] = ob[i, d, 8:24, :] + section_weight * rate
+
+    for d in range(16):
+        bulk = jnp.full((16, 64), (-2.0 * step_size) * med[0, d], F32)
+        light = jnp.full((16, 64), (-2.0 * step_size) * med[1, d], F32)
+        rate_p = opre[d] + bulk * dx_ocean(1, d)
+        ocean_out(1, d, light * dx_ocean(0, d))
+        if d < 15:
+            ocean_out(0, d, rate_p)
+
+    for e in (-1, 1):
+        when(has[e], lambda: plane_wait(0, e))
+        when(has_late[e], lambda: merge(e))
+
+    window = plane[0].reshape(24, 128)
+    bed_speed = lax.dot_general(
+        blend_x, window, (((0,), (0,)), ((), ())), precision=HIGHEST, preferred_element_type=F32
+    )
+    bed_speed = jnp.dot(bed_speed, blend_y, precision=HIGHEST, preferred_element_type=F32)
+
+    bulk = jnp.full((16, 64), (step_size * inv_norm) * med[0, 15], F32)
+    ocean_out(0, 15, rate_p + bulk * (ov[1, 15] - bed_speed))
+
+    sent(x_up, *up_copies, wave_up)
+    sent(x_down, *down_copies, wave_down)
+    for e in (-1, 1):
+        sent(has_late[e], plane_on[e])
+    sent(y_up, ys_copies[0])
+    sent(y_down, ys_copies[1])
+    sent(has_right, yo_copies[0])
+    sent(has_left, yo_copies[1])
+    sent(z_up, *z_up_copies)
+    sent(z_down, *z_down_copies)
+    for pred, copies in plane_late:
+        sent(pred, *copies)
+    for pred, copies in plane_early:
+        sent(pred, *copies)
+    for k in range(1, nz):
+        sent(gz == k, coarse_copies[k - 1])
+
+
+def finish_kernel(nx, o_next, o_rate, sb, mb, txs, dys, dzs, s_next_out, s_rate_out, o_next_out, o_rate_out, s_next, s_rate, sem):
+    copies = [
+        pltpu.make_async_copy(o_next, o_next_out, sem.at[0]),
+        pltpu.make_async_copy(o_rate, o_rate_out, sem.at[1]),
+    ]
+    for copy in copies:
+        copy.start()
+    gx = lax.axis_index("gx")
+    sub = lax.broadcasted_iota(jnp.int32, (8, 128), 0)
+    wx = weights(sub, 8, gx == 0, gx == nx - 1, False)
 
     def dx(i, f, z):
         out = txs[i, z]
@@ -496,78 +576,11 @@
         for f in range(9):
             s_rate[f, z] = rates[f]
             s_next[f, z] = own[f] + section_weight * rates[f]
-
-    pos = lax.broadcasted_iota(jnp.int32, (16, 64), 0)
-    wp = weights(pos, 16, x_first, x_last, False)
-    far_up, far_down = wp[3] != 0.0, wp[-3] != 0.0
-
-    def dx_ocean(i, d):
-        out = total(wp[k] * ob[i, d, 8 + k : 24 + k, :] for k in range(-2, 3))
-        out = out + wp[3] * jnp.where(far_up, ob[i, d, 11:27, :], 0.0)
-        return out + wp[-3] * jnp.where(far_down, ob[i, d, 5:21, :], 0.0)
-
-    def ocean_out(i, d, rate):
-        o_rate[i, d] = rate
-        o_next[i, d] = ob[i, d, 8:24, :] + section_weight * rate
-
-    for d in range(16):
-        bulk = jnp.full((16, 64), (-2.0 * step_size) * med[0, d], F32)
-        light = jnp.full((16, 64), (-2.0 * step_size) * med[1, d], F32)
-        rate_p = opre[d] + bulk * dx_ocean(1, d)
-        ocean_out(1, d, light * dx_ocean(0, d))
-        if d < 15:
-            ocean_out(0, d, rate_p)
-
-    loads[5].wait()
-    loads[6].wait()
-    for e in (-1, 1):
-        when(has[e], lambda: plane_wait(0, e))
-        when(has_late[e], lambda: merge(e))
-
-    window = plane[0].reshape(24, 128)
-    fine_x = lax.broadcasted_iota(jnp.int32, (24, 16), 1)
-    coarse_x = lax.broadcasted_iota(jnp.int32, (24, 16), 0) + (8 * gx - 8)
-    near_x = 8 * gx + fine_x // 2
-    far_x = jnp.clip(near_x + ox[...], 0, 8 * nx - 1)
-    blend_x = jnp.where(coarse_x == near_x, 0.75, 0.0) + jnp.where(coarse_x == far_x, 0.25, 0.0)
-    fine_y = lax.broadcasted_iota(jnp.int32, (128, 64), 1)
-    coarse_y = lax.broadcasted_iota(jnp.int32, (128, 64), 0)
-    near_y = 128 * gy + 32 * gz + fine_y // 2
-    far_y = jnp.clip(near_y + oy[...], 0, 128 * ny - 1)
-    blend_y = jnp.where(coarse_y == lax.rem(near_y, 128), 0.75, 0.0)
-    blend_y = blend_y + jnp.where(coarse_y == lax.rem(far_y, 128), 0.25, 0.0)
-    bed_speed = lax.dot_general(
-        blend_x, window, (((0,), (0,)), ((), ())), precision=HIGHEST, preferred_element_type=F32
-    )
-    bed_speed = jnp.dot(bed_speed, blend_y, precision=HIGHEST, preferred_element_type=F32)
-
-    bulk = jnp.full((16, 64), (step_size * inv_norm) * med[0, 15], F32)
-    ocean_out(0, 15, rate_p + bulk * (ov[1, 15] - bed_speed))
-
-    sent(x_up, *up_copies, wave_up)
-    sent(x_down, *down_copies, wave_down)
-    for e in (-1, 1):
-        sent(has_late[e], plane_on[e])
-    sent(y_up, ys_copies[0])
-    sent(y_down, ys_copies[1])
-    sent(has_right, yo_copies[0])
-    sent(has_left, yo_copies[1])
-    sent(z_up, *z_up_copies)
-    sent(z_down, *z_down_copies)
-    for pred, copies in plane_late:
-        sent(pred, *copies)
-    for pred, copies in plane_early:
-        sent(pred, *copies)
-    for k in range(1, nz):
-        sent(gz == k, coarse_copies[k - 1])
-
-
-def write_kernel(*refs):
-    count = (len(refs) - 1) // 2
-    sem = refs[-1]
-    copies = [pltpu.make_async_copy(refs[i], refs[count + i], sem.at[i]) for i in range(count)]
-    for copy in copies:
-        copy.start()
+        if z % 2 == 1:
+            for i, (held, out) in enumerate(((s_next, s_next_out), (s_rate, s_rate_out))):
+                copy = pltpu.make_async_copy(held.at[:, z - 1 : z + 1], out.at[:, z - 1 : z + 1], sem.at[1 + z + i])
+                copy.start()
+                copies.append(copy)
     for copy in copies:
         copy.wait()
 
@@ -577,16 +590,17 @@
     v = lambda *shape: pltpu.VMEM(shape, F32)
     held = pl.pallas_call(
         functools.partial(section_kernel, sizes),
-        out_shape=[pltpu.VMEM(shape, F32) for shape in outs],
+        out_shape=[pltpu.VMEM(shape, F32) for shape in outs[2:]]
+        + [v(9, 8, 24, 128), v(4, 8, 8, 128), v(6, 8, 8, 128), v(6, 8, 8, 128), v(6, 8, 8, 128)],
         in_specs=[pl.BlockSpec(memory_space=pltpu.HBM)] * 6,
-        out_specs=[pl.BlockSpec(memory_space=pltpu.VMEM)] * 4,
+        out_specs=[pl.BlockSpec(memory_space=pltpu.VMEM)] * 7,
         scratch_shapes=[
-            v(9, 8, 24, 128), v(4, 8, 8, 128), v(2, 16, 32, 64), v(2, 16, 16, 64),
+            v(2, 16, 32, 64), v(2, 16, 16, 64),
             pltpu.SMEM((2, 16), F32), pltpu.VMEM((1, 16), jnp.int32), pltpu.VMEM((1, 64), jnp.int32),
             v(6, 2, 8, 128), v(6, 2, 8, 128), v(2, 3, 8, 128), v(4, 8, 128),
             v(2, 16, 2, 128), v(16, 2, 128), v(16, 2, 128),
             v(2, 8, 128), v(2, 8, 128), v(2, 8, 128), v(2, 8, 128), v(2, 8, 128), v(2, 8, 128), v(8, 128),
-            v(6, 8, 8, 128), v(2, 16, 8, 128), v(6, 8, 8, 128), v(6, 8, 8, 128), v(16, 16, 64), v(2, 16, 8, 128),
+            v(2, 16, 8, 128), v(16, 16, 64), v(2, 16, 8, 128),
             pltpu.SemaphoreType.DMA((8,)), pltpu.SemaphoreType.DMA((64,)), pltpu.SemaphoreType.DMA((24,)),
             pltpu.SemaphoreType.REGULAR((8,)),
         ],
@@ -599,13 +613,13 @@
         for a in (solid_state, material, ocean_state, ocean_medium, offset_x.reshape(1, -1), offset_y.reshape(1, -1))
     ))
     return pl.pallas_call(
-        write_kernel,
+        functools.partial(finish_kernel, sizes[0]),
         out_shape=[jax.ShapeDtypeStruct(shape, F32) for shape in outs],
-        in_specs=[pl.BlockSpec(memory_space=pltpu.VMEM)] * 4,
+        in_specs=[pl.BlockSpec(memory_space=pltpu.VMEM)] * 7,
         out_specs=[pl.BlockSpec(memory_space=pl.ANY)] * 4,
-        scratch_shapes=[pltpu.SemaphoreType.DMA((4,))],
+        scratch_shapes=[v(*outs[0]), v(*outs[0]), pltpu.SemaphoreType.DMA((10,))],
         compiler_params=pltpu.CompilerParams(vmem_limit_bytes=4 * 2**20),
-        name="write_out",
+        name="finish",
     )(*held)
 
 

time: 14.1 us -> 14.1 us (level)
  no operation moved by 1% of the time
where the time goes in v5:
time: 14.1 us; the launch traced here: 14 us
  Pallas kernels  13.3 us (94%)
  between operations  0.64 us (5%)
    pallas_call x1, Pallas kernels, body(): pl.pallas_call(functools.partial(section_kernel, sizes), out_shape=[pltpu...  12.1 us
    pallas_call x1, Pallas kernels, body(): pl.pallas_call(functools.partial(finish_kernel, sizes[0]), out_shape=[jax...  1.24 us

profile of v5, /device:TPU:14, one launch (start us, length us, event | category | flops | bytes accessed | tf_op | source)
XLA Modules:
  0.0 14.0 jit_solution(8563812900993126668)
XLA Ops:
  0.6 12.1 %section.1 = (f32[4,16,16,64]{3,2,1,0:T(8,128)S(1)}, f32[4,16,16,64]{3,2,1,0:T(8,128)S(1)}, f32[9,8,24,128]{3,2,1,0:T(8,128)S(1)}, f32[4,8,8,128]{3,2,1,0:T(8,12...) custom-call(f32[9,8,8,128]{3,2,1,0:T(8,128)} %solid.1, ...), custom_call_target="tpu_custom_call" | custom-call | tf_op jit(solution)/shard_map/section/pallas_call | solution.py:591
  12.7 1.2 %finish.1 = (f32[9,8,8,128]{3,2,1,0:T(8,128)}, f32[9,8,8,128]{3,2,1,0:T(8,128)}, f32[4,16,16,64]{3,2,1,0:T(8,128)}, f32[4,16,16,64]{3,2,1,0:T(8,128)}) custom-call(f32[4,16,16,64]{3,2,1,0:T(8,128)S(1)} %get-tuple-element.11.o_next, f32[4,16,16,64]{3,2,1,0:T(8,128)S(1)} %get-tuple-element.12.o_rate, f32[9,8,24,128]{3,2,1,0:T(8,128)S(1)} %get-tuple-element.13.sb, ...), custom_call_target="tpu_custom_call" | custom-call | tf_op jit(solution)/shard_map/finish/pallas_call | solution.py:615

commit v6 on v5

--- a/solution.py
+++ b/solution.py
@@ -213,12 +213,6 @@
     n_greet = count(y_down_near, even) + jnp.where(gz == 2, 2, 0)
     n_greet = n_greet + n_early * (1 + jnp.where(z_first, nz - 1 + n_y, 0))
     when(n_greet > 0, lambda: pl.semaphore_wait(barrier, n_greet))
-    for e, index in ((1, 1), (-1, 0)):
-        when(has_early[e], lambda: tell(index, xs[e], gy, gz))
-    when(y_down_near, lambda: tell(2, gx, down_y, gz))
-    when(gz == 2, lambda: tell(3, gx, gy, 1))
-    when(even, lambda: tell(4, gx, gy, gz + 1))
-    when(gz == 2, lambda: tell(5, gx, gy, 0))
     def await_partner(pred, index, amount=1):
         when(pred, lambda: pl.semaphore_wait(there.at[index], amount))
 
@@ -238,6 +232,12 @@
     wave_down = remote(xo_out.at[0], xo_high, 5, (down_x, gy, gz))
     start(has_early[1], up_copies[0])
     start(has_early[-1], down_copies[0])
+    for e, index in ((1, 1), (-1, 0)):
+        when(has_early[e], lambda: tell(index, xs[e], gy, gz))
+    when(y_down_near, lambda: tell(2, gx, down_y, gz))
+    when(gz == 2, lambda: tell(3, gx, gy, 1))
+    when(even, lambda: tell(4, gx, gy, gz + 1))
+    when(gz == 2, lambda: tell(5, gx, gy, 0))
 
     z_up_copies = [
         remote(solid.at[a : a + 3, 6:8], z_low.at[b : b + 3], 6 + i, (gx, gy, gz + 1))

time: 14.1 us -> 14.1 us (level)
  no operation moved by 1% of the time
where the time goes in v6:
time: 14.1 us; the launch traced here: 14 us
  Pallas kernels  13.3 us (94%)
  between operations  0.64 us (5%)
    pallas_call x1, Pallas kernels, body(): pl.pallas_call(functools.partial(section_kernel, sizes), out_shape=[pltpu...  12.1 us
    pallas_call x1, Pallas kernels, body(): pl.pallas_call(functools.partial(finish_kernel, sizes[0]), out_shape=[jax...  1.24 us

profile of v6, /device:TPU:14, one launch (start us, length us, event | category | flops | bytes accessed | tf_op | source)
XLA Modules:
  0.0 14.0 jit_solution(15937507267114161745)
XLA Ops:
  0.6 12.1 %section.1 = (f32[4,16,16,64]{3,2,1,0:T(8,128)S(1)}, f32[4,16,16,64]{3,2,1,0:T(8,128)S(1)}, f32[9,8,24,128]{3,2,1,0:T(8,128)S(1)}, f32[4,8,8,128]{3,2,1,0:T(8,12...) custom-call(f32[9,8,8,128]{3,2,1,0:T(8,128)} %solid.1, ...), custom_call_target="tpu_custom_call" | custom-call | tf_op jit(solution)/shard_map/section/pallas_call | solution.py:591
  12.7 1.2 %finish.1 = (f32[9,8,8,128]{3,2,1,0:T(8,128)}, f32[9,8,8,128]{3,2,1,0:T(8,128)}, f32[4,16,16,64]{3,2,1,0:T(8,128)}, f32[4,16,16,64]{3,2,1,0:T(8,128)}) custom-call(f32[4,16,16,64]{3,2,1,0:T(8,128)S(1)} %get-tuple-element.11.o_next, f32[4,16,16,64]{3,2,1,0:T(8,128)S(1)} %get-tuple-element.12.o_rate, f32[9,8,24,128]{3,2,1,0:T(8,128)S(1)} %get-tuple-element.13.sb, ...), custom_call_target="tpu_custom_call" | custom-call | tf_op jit(solution)/shard_map/finish/pallas_call | solution.py:615

commit v7 on v5

--- a/solution.py
+++ b/solution.py
@@ -576,9 +576,9 @@
         for f in range(9):
             s_rate[f, z] = rates[f]
             s_next[f, z] = own[f] + section_weight * rates[f]
-        if z % 2 == 1:
+        if z % 4 == 3:
             for i, (held, out) in enumerate(((s_next, s_next_out), (s_rate, s_rate_out))):
-                copy = pltpu.make_async_copy(held.at[:, z - 1 : z + 1], out.at[:, z - 1 : z + 1], sem.at[1 + z + i])
+                copy = pltpu.make_async_copy(held.at[:, z - 3 : z + 1], out.at[:, z - 3 : z + 1], sem.at[1 + z + i])
                 copy.start()
                 copies.append(copy)
     for copy in copies:

time: 14.1 us -> 14.1 us (level)
  no operation moved by 1% of the time
where the time goes in v7:
time: 14.1 us; the launch traced here: 14 us
  Pallas kernels  13.3 us (94%)
  between operations  0.64 us (5%)
    pallas_call x1, Pallas kernels, body(): pl.pallas_call(functools.partial(section_kernel, sizes), out_shape=[pltpu...  12.1 us
    pallas_call x1, Pallas kernels, body(): pl.pallas_call(functools.partial(finish_kernel, sizes[0]), out_shape=[jax...  1.24 us

profile of v7, /device:TPU:14, one launch (start us, length us, event | category | flops | bytes accessed | tf_op | source)
XLA Modules:
  0.0 14.0 jit_solution(9877808763494982352)
XLA Ops:
  0.6 12.1 %section.1 = (f32[4,16,16,64]{3,2,1,0:T(8,128)S(1)}, f32[4,16,16,64]{3,2,1,0:T(8,128)S(1)}, f32[9,8,24,128]{3,2,1,0:T(8,128)S(1)}, f32[4,8,8,128]{3,2,1,0:T(8,12...) custom-call(f32[9,8,8,128]{3,2,1,0:T(8,128)} %solid.1, ...), custom_call_target="tpu_custom_call" | custom-call | tf_op jit(solution)/shard_map/section/pallas_call | solution.py:591
  12.7 1.2 %finish.1 = (f32[9,8,8,128]{3,2,1,0:T(8,128)}, f32[9,8,8,128]{3,2,1,0:T(8,128)}, f32[4,16,16,64]{3,2,1,0:T(8,128)}, f32[4,16,16,64]{3,2,1,0:T(8,128)}) custom-call(f32[4,16,16,64]{3,2,1,0:T(8,128)S(1)} %get-tuple-element.11.o_next, f32[4,16,16,64]{3,2,1,0:T(8,128)S(1)} %get-tuple-element.12.o_rate, f32[9,8,24,128]{3,2,1,0:T(8,128)S(1)} %get-tuple-element.13.sb, ...), custom_call_target="tpu_custom_call" | custom-call | tf_op jit(solution)/shard_map/finish/pallas_call | solution.py:615
